TPU v7x, 512 devices: a whole 4x8x8 slice. The times are simulated.
512 devices in a mesh: tm: 16 (over y_lo, x, core), mp: 8 (over z), dp: 4 (over y_hi).
Axes of the slice: x: 4, y: 8 (y_hi: 4, y_lo: 2; y = y_hi * 2 + y_lo), z: 8, core: 2. Of those that a mesh axis runs over, the one named last changes fastest.
Arguments:
- q_proj: bfloat16 [4, 6144, 5120], P('dp', 'tm', 'mp'), may hold values from -80 to 80
- k_proj: bfloat16 [4, 6144, 5120], P('dp', 'tm', 'mp'), may hold values from -80 to 80
- values: bfloat16 [4, 6144, 5120], P('dp', 'tm', 'mp'), may hold values from -6 to 6
- grad_out: bfloat16 [4, 6144, 5120], P('dp', 'tm', 'mp'), may hold values from -48 to 48
- gain_q: float32 [5120], P('mp'), may hold values from 0.5 to 1.5
- gain_k: float32 [5120], P('mp'), may hold values from 0.5 to 1.5
- valid_count: int32 [4, 16], P('dp', 'tm'), may hold values from 192 to 384, as said below
- segment: int32 [4, 16], P('dp', 'tm'), may hold values from 0 to 3, never falling along the last dimension, each value on 1 to 8 neighbouring positions
Outputs:
- query_grad: bfloat16 [4, 6144, 5120], P('dp', 'tm', 'mp')
- key_grad: bfloat16 [4, 6144, 5120], P('dp', 'tm', 'mp')
- value_grad: bfloat16 [4, 6144, 5120], P('dp', 'tm', 'mp')
- gain_q_grad: float32 [5120], P('mp')
- gain_k_grad: float32 [5120], P('mp')
Inputs may be any that keep to these rules, and one draw needn't show every extreme that they name: `valid_count`: the valid tokens of a group are its first slots; some group is full. `segment`: along a rollout the scene ids never fall, start at 0 and skip none; a scene spans at most 8 groups.
All inputs are finite; a program needn't handle non-finite values.
Results may differ from a plain program's by a relative error of at most 0.011.
Values may be sent and summed in bfloat16 or wider, within the bound.
No kernel may reach another device: no remote copies, remote signals or barrier semaphores. Data moves between devices by JAX's collectives and lax.ppermute only.
A program may use at most 64 MiB of HBM per device.

v0:
```python
import math

import jax
import jax.numpy as jnp
from jax import lax
from jax.sharding import PartitionSpec as P

HEADS = 40
HD = 128
WIN = 3


EPSILON = 1e-06


def shifted(value, axis, steps):
    count = lax.axis_size(axis)
    leading, last = (max(0, -steps), min(count, count - steps))
    return lax.ppermute(value, axis, [(source, source + steps) for source in range(leading, last)])


def head_cols(matrix, head_index, head_size):
    return lax.dynamic_slice_in_dim(matrix, head_index * head_size, head_size, 2)


def put_cols(matrix, new_block, head_index, head_size):
    return lax.dynamic_update_slice_in_dim(matrix, new_block, head_index * head_size, 2)


def on_device(q_proj, k_proj, values, grad_out, gain_q, gain_k, valid_count, segment):
    roll_count, slot_count, local_width = q_proj.shape
    head_size = HD
    local_heads = local_width // head_size
    full_width = HEADS * HD
    root_size = math.sqrt(head_size)
    q_wide = q_proj.astype(jnp.float32)
    k_wide = k_proj.astype(jnp.float32)
    q_power, k_power = lax.psum(
        (jnp.sum(q_wide * q_wide, axis=-1), jnp.sum(k_wide * k_wide, axis=-1)), "mp"
    )
    q_root = jnp.sqrt(q_power / full_width + EPSILON)[:, :, None]
    k_root = jnp.sqrt(k_power / full_width + EPSILON)[:, :, None]
    q_unit = q_wide / q_root
    k_unit = k_wide / k_root
    q_norm = (q_unit * gain_q).astype(jnp.bfloat16)
    k_norm = (k_unit * gain_k).astype(jnp.bfloat16)
    slot_ids = jnp.arange(slot_count, dtype=jnp.int32)
    is_live = slot_ids[None, :] < valid_count
    own_tag = (segment + 1).astype(jnp.bfloat16)
    key_tag = jnp.where(is_live, own_tag, jnp.zeros_like(own_tag))
    grad_live = jnp.where(is_live[:, :, None], grad_out, jnp.zeros_like(grad_out))
    blocks = [(k_norm, values, key_tag)]
    for distance in range(1, WIN + 1):
        blocks.append(shifted((k_norm, values, key_tag), "tm", distance))
    keys_all = jnp.concatenate([member[0] for member in blocks], axis=1)
    values_all = jnp.concatenate([member[1] for member in blocks], axis=1)
    allowed = jnp.concatenate([member[2] for member in blocks], axis=1) == own_tag
    key_rows = keys_all.shape[1]

    def query_head(head_index, carried):
        q_grad, k_grad, v_grad, row_maxes, row_sums, row_deltas = carried
        q_head = head_cols(q_norm, head_index, head_size)
        k_head = head_cols(keys_all, head_index, head_size)
        v_head = head_cols(values_all, head_index, head_size)
        g_head = head_cols(grad_live, head_index, head_size)
        scores = (
            jnp.einsum("rqd,rkd->rqk", q_head, k_head, preferred_element_type=jnp.float32)
            / root_size
        )
        scores = jnp.where(allowed[:, None, :], scores, -jnp.inf)
        row_max = jnp.max(scores, axis=-1, keepdims=True)
        exponent = jnp.exp(scores - row_max)
        row_sum = jnp.sum(exponent, axis=-1, keepdims=True)
        weights = exponent / row_sum
        grad_weights = jnp.einsum(
            "rqd,rkd->rqk", g_head, v_head, preferred_element_type=jnp.float32
        )
        row_delta = jnp.sum(weights * grad_weights, axis=-1, keepdims=True)
        grad_scores = (weights * (grad_weights - row_delta)).astype(jnp.bfloat16)
        q_part = (
            jnp.einsum("rqk,rkd->rqd", grad_scores, k_head, preferred_element_type=jnp.float32)
            / root_size
        )
        k_part = (
            jnp.einsum("rqk,rqd->rkd", grad_scores, q_head, preferred_element_type=jnp.float32)
            / root_size
        )
        v_part = jnp.einsum(
            "rqk,rqd->rkd", weights.astype(jnp.bfloat16), g_head, preferred_element_type=jnp.float32
        )
        return (
            put_cols(q_grad, q_part, head_index, head_size),
            put_cols(k_grad, k_part, head_index, head_size),
            put_cols(v_grad, v_part, head_index, head_size),
            lax.dynamic_update_slice_in_dim(row_maxes, row_max, head_index, 2),
            lax.dynamic_update_slice_in_dim(row_sums, row_sum, head_index, 2),
            lax.dynamic_update_slice_in_dim(row_deltas, row_delta, head_index, 2),
        )

    stat_zeros = jnp.zeros((roll_count, slot_count, local_heads), jnp.float32)
    initial = (
        jnp.zeros((roll_count, slot_count, local_width), jnp.float32),
        jnp.zeros((roll_count, key_rows, local_width), jnp.float32),
        jnp.zeros((roll_count, key_rows, local_width), jnp.float32),
        stat_zeros,
        stat_zeros,
        stat_zeros,
    )
    q_grad, k_grad, v_grad, row_maxes, row_sums, row_deltas = lax.fori_loop(
        0, local_heads, query_head, initial
    )
    k_own = k_grad[:, :slot_count]
    v_own = v_grad[:, :slot_count]
    for distance in range(1, WIN + 1):
        rows_from = distance * slot_count
        back_k, back_v = shifted(
            (
                k_grad[:, rows_from : rows_from + slot_count],
                v_grad[:, rows_from : rows_from + slot_count],
            ),
            "tm",
            -distance,
        )
        k_own = k_own + back_k
        v_own = v_own + back_v
    q_scaled = q_grad * gain_q
    k_scaled = k_own * gain_k
    q_inner, k_inner = lax.psum(
        (jnp.sum(q_scaled * q_unit, axis=-1), jnp.sum(k_scaled * k_unit, axis=-1)), "mp"
    )
    query_grad = ((q_scaled - q_unit * (q_inner / full_width)[:, :, None]) / q_root).astype(
        jnp.bfloat16
    )
    key_grad = ((k_scaled - k_unit * (k_inner / full_width)[:, :, None]) / k_root).astype(
        jnp.bfloat16
    )
    gain_q_grad, gain_k_grad = lax.psum(
        (jnp.sum(q_grad * q_unit, axis=(0, 1)), jnp.sum(k_own * k_unit, axis=(0, 1))), ("tm", "dp")
    )
    return (query_grad, key_grad, v_own.astype(jnp.bfloat16), gain_q_grad, gain_k_grad)


def solution(mesh):
    in_specs = (
        P("dp", "tm", "mp"),
        P("dp", "tm", "mp"),
        P("dp", "tm", "mp"),
        P("dp", "tm", "mp"),
        P("mp"),
        P("mp"),
        P("dp", "tm"),
        P("dp", "tm"),
    )
    out_specs = (P("dp", "tm", "mp"), P("dp", "tm", "mp"), P("dp", "tm", "mp"), P("mp"), P("mp"))
    return jax.shard_map(
        on_device, mesh=mesh, in_specs=in_specs, out_specs=out_specs, check_vma=False
    )
```

profile of v0, /device:TPU:72, one launch (start us, length us, event | category | flops | bytes accessed | tf_op | source)
XLA Modules:
  0.0 453.0 jit_solution(10086278122426587737)
XLA Ops:
  2.0 2.8 collective-permute-start.2
  4.9 3.4 collective-permute-start.1
  10.7 20.2 %all-reduce.2 = (f32[1,384]{1,0:T(1,128)S(1)}, f32[1,384]{1,0:T(1,128)S(1)}) all-reduce(f32[1,384]{1,0:T(1,128)S(1)} %reduce_sum.85, f32[1,384]{1,0:T(1,128)S(1)} %reduce_sum.87), channel_id=1, replica_groups=mesh['tm'=16,'mp'=8,'dp'=4] {'mp'}, use_global_device_ids=true, to_apply=%region_1.0 | all-reduce | flops 768 | bytes 6144 | tf_op jit(solution)/shard_map/psum | solution.py:38
  30.9 1.2 multiply_convert_fusion.1
  32.1 1.9 collective-permute-start.5
  34.1 3.1 collective-permute-start.4
  37.2 2.1 collective-permute-start.3
  41.5 1.9 collective-permute-start
  43.4 1.9 collective-permute-start.7
  45.4 25.2 %collective-permute-done = bf16[1,384]{1,0:T(2,128)(2,1)S(1)} collective-permute-done((bf16[1,384]{1,0:T(2,128)(2,1)S(1)}, bf16[1,384]{1,0:T(2,128)(2,1)S(1)}, u32[]{:S(2)}, u32[]{:S(2)}) %collective-permute-start) | collective-permute-done | bytes 800 | tf_op jit(solution)/shard_map/ppermute | solution.py:19
  70.5 1.9 collective-permute-start.6
  72.5 1.9 collective-permute-start.8
  75.2 1.5 pad_maximum_fusion
  76.7 15.8 %collective-permute-done.6 = bf16[1,384,640]{2,1,0:T(8,128)(2,1)S(1)} collective-permute-done((bf16[1,384,640]{2,1,0:T(8,128)(2,1)}, bf16[1,384,640]{2,1,0:T(8,128)(2,1)S(1)}, u32[]{:S(2)}, u32[]{:S(2)}) %collective-permute-start.6) | collective-permute-done | bytes 491552 | tf_op jit(solution)/shard_map/ppermute | solution.py:19
  92.5 2.6 pad_maximum_fusion.1
  95.1 2.2 broadcast.133.clone
  97.3 2.1 broadcast.133
  99.4 40.5 %while.17 = (s32[]{:T(128)}, f32[1,384,640]{2,1,0:T(8,128)S(1)}, f32[1,1536,640]{2,1,0:T(8,128)}, f32[1,1536,640]{2,1,0:T(8,128)}, pred[1,1536]{1,0:T(4,128)(4,1...) while((s32[]{:T(128)}, f32[1,384,640]{2,1,0:T(8,128)S(1)}, ...), condition=%wide.region_8.9_spmd, body=%wide.region_4.8_spmd.sunk | while | flops 765246336 | bytes 23423668 | solution.py:109
  100.5 1.8 multiply_reduce_fusion.8
  103.4 2.6 fusion.58
  106.0 1.5 fusion.57
  108.6 1.8 multiply_reduce_fusion.8
  111.5 2.7 fusion.58
  114.2 1.5 fusion.57
  116.8 1.8 multiply_reduce_fusion.8
  119.7 2.7 fusion.58
  122.4 1.5 fusion.57
  124.9 1.8 multiply_reduce_fusion.8
  127.8 2.6 fusion.58
  130.5 1.4 fusion.57
  133.0 1.8 multiply_reduce_fusion.8
  135.9 2.6 fusion.58
  138.5 1.5 fusion.57
  140.0 2.1 fusion.34
  142.1 7.7 %collective-permute-start.9 = (f32[1,384,640]{2,1,0:T(8,128)S(1)}, f32[1,384,640]{2,1,0:T(8,128)S(1)}, u32[]{:S(2)}, u32[]{:S(2)}) collective-permute-start(f32[1,384,640]{2,1,0:T(8,128)S(1)} %get-tuple-element.200), channel_id=1, source_target_pairs={{32,0},{64,32},{96,64},{128,96},{160,128},{192,160},{224,192},{256... | collective-permute-start | bytes 2949128 | tf_op jit(solution)/shard_map/ppermute | solution.py:19
  149.8 1.9 collective-permute-start.11
  151.7 1.9 collective-permute-start.10
  154.1 1.7 fusion.33
  155.8 1.9 collective-permute-start.12
  157.7 1.9 collective-permute-start.14
  159.7 33.3 %collective-permute-done.9 = f32[1,384,640]{2,1,0:T(8,128)S(1)} collective-permute-done((f32[1,384,640]{2,1,0:T(8,128)S(1)}, f32[1,384,640]{2,1,0:T(8,128)S(1)}, u32[]{:S(2)}, u32[]{:S(2)}) %collective-permute-start.9) | collective-permute-done | bytes 983072 | tf_op jit(solution)/shard_map/ppermute | solution.py:19
  193.0 1.9 collective-permute-start.13
  194.9 19.2 %collective-permute-done.11 = f32[1,384,640]{2,1,0:T(8,128)S(1)} collective-permute-done((f32[1,384,640]{2,1,0:T(8,128)S(1)}, f32[1,384,640]{2,1,0:T(8,128)S(1)}, u32[]{:S(2)}, u32[]{:S(2)}) %collective-permute-start.11) | collective-permute-done | bytes 983072 | tf_op jit(solution)/shard_map/ppermute | solution.py:19
  214.1 22.1 %collective-permute-done.10 = f32[1,384,640]{2,1,0:T(8,128)S(1)} collective-permute-done((f32[1,384,640]{2,1,0:T(8,128)S(1)}, f32[1,384,640]{2,1,0:T(8,128)S(1)}, u32[]{:S(2)}, u32[]{:S(2)}) %collective-permute-start.10) | collective-permute-done | bytes 983072 | tf_op jit(solution)/shard_map/ppermute | solution.py:19
  236.2 1.7 multiply_reduce_fusion.1
  238.0 193.0 %all-reduce = (f32[640]{0:T(1024)}, f32[640]{0:T(1024)}) all-reduce(f32[640]{0:T(1024)S(1)} %get-tuple-element.166, f32[640]{0:T(1024)S(1)} %get-tuple-element.164), channel_id=1, replica_groups=mesh['tm'=16,'mp'=8,'dp'=4] {'tm','dp'}, use_global_device_ids=true, to_apply=%region_14.15 | all-reduce | flops 1280 | bytes 10240 | tf_op jit(solution)/shard_map/psum | solution.py:137
  431.0 16.8 %all-reduce.1 = (f32[1,384]{1,0:T(1,128)S(1)}, f32[1,384]{1,0:T(1,128)S(1)}) all-reduce(f32[1,384]{1,0:T(1,128)S(1)} %reduce_sum.89, f32[1,384]{1,0:T(1,128)S(1)} %reduce_sum.91), channel_id=1, replica_groups=mesh['tm'=16,'mp'=8,'dp'=4] {'mp'}, use_global_device_ids=true, to_apply=%region_10.11 | all-reduce | flops 768 | bytes 6144 | tf_op jit(solution)/shard_map/psum | solution.py:128
  450.0 3.0 add_convert_fusion
  (71 shorter events, 19.1 us)
Async XLA Ops:
  0.6 39.9 %copy-start.3 = (bf16[1,384,640]{2,1,0:T(8,128)(2,1)S(1)}, bf16[1,384,640]{2,1,0:T(8,128)(2,1)}, u32[]{:S(2)}) copy-start(bf16[1,384,640]{2,1,0:T(8,128)(2,1)} %param.13) | copy-start | bytes 1474564
  2.0 39.5 %collective-permute-start.2 = (bf16[1,384]{1,0:T(2,128)(2,1)S(1)}, bf16[1,384]{1,0:T(2,128)(2,1)S(1)}, u32[]{:S(2)}, u32[]{:S(2)}) collective-permute-start(bf16[1,384]{1,0:T(2,128)(2,1)S(1)} %compare_select_fusion), channel_id=1, source_target_pairs={{0,96},{32,128},{64,160},{96,192},{128,224},{160,256},{192,288},{2... | collective-permute-start | bytes 2312 | tf_op jit(solution)/shard_map/ppermute | solution.py:19
  4.9 38.6 %collective-permute-start.1 = (bf16[1,384]{1,0:T(2,128)(2,1)S(1)}, bf16[1,384]{1,0:T(2,128)(2,1)S(1)}, u32[]{:S(2)}, u32[]{:S(2)}) collective-permute-start(bf16[1,384]{1,0:T(2,128)(2,1)S(1)} %compare_select_fusion), channel_id=1, source_target_pairs={{0,64},{32,96},{64,128},{96,160},{128,192},{160,224},{192,256},{22... | collective-permute-start | bytes 2312 | tf_op jit(solution)/shard_map/ppermute | solution.py:19
  32.1 40.3 %collective-permute-start.5 = (bf16[1,384,640]{2,1,0:T(8,128)(2,1)S(1)}, bf16[1,384,640]{2,1,0:T(8,128)(2,1)S(1)}, u32[]{:S(2)}, u32[]{:S(2)}) collective-permute-start(bf16[1,384,640]{2,1,0:T(8,128)(2,1)S(1)} %multiply_convert_fusion.1), channel_id=1, source_target_pairs={{0,96},{32,128},{64,160},{96,192},{128,224},{160,256},{192,288},{2... | collective-permute-start | bytes 1474568 | tf_op jit(solution)/shard_map/ppermute | solution.py:19
  34.1 40.4 %collective-permute-start.4 = (bf16[1,384,640]{2,1,0:T(8,128)(2,1)S(1)}, bf16[1,384,640]{2,1,0:T(8,128)(2,1)S(1)}, u32[]{:S(2)}, u32[]{:S(2)}) collective-permute-start(bf16[1,384,640]{2,1,0:T(8,128)(2,1)S(1)} %multiply_convert_fusion.1), channel_id=1, source_target_pairs={{0,64},{32,96},{64,128},{96,160},{128,192},{160,224},{192,256},{22... | collective-permute-start | bytes 1474568 | tf_op jit(solution)/shard_map/ppermute | solution.py:19
  37.2 38.1 %collective-permute-start.3 = (bf16[1,384,640]{2,1,0:T(8,128)(2,1)S(1)}, bf16[1,384,640]{2,1,0:T(8,128)(2,1)}, u32[]{:S(2)}, u32[]{:S(2)}) collective-permute-start(bf16[1,384,640]{2,1,0:T(8,128)(2,1)S(1)} %multiply_convert_fusion.1), channel_id=1, source_target_pairs={{0,32},{32,64},{64,96},{96,128},{128,160},{160,192},{192,224},{224... | collective-permute-start | bytes 1474568 | tf_op jit(solution)/shard_map/ppermute | solution.py:19
  41.5 29.0 %collective-permute-start = (bf16[1,384]{1,0:T(2,128)(2,1)S(1)}, bf16[1,384]{1,0:T(2,128)(2,1)S(1)}, u32[]{:S(2)}, u32[]{:S(2)}) collective-permute-start(bf16[1,384]{1,0:T(2,128)(2,1)S(1)} %compare_select_fusion), channel_id=1, source_target_pairs={{0,32},{32,64},{64,96},{96,128},{128,160},{160,192},{192,224},{224... | collective-permute-start | bytes 2312 | tf_op jit(solution)/shard_map/ppermute | solution.py:19
  43.4 33.3 %collective-permute-start.7 = (bf16[1,384,640]{2,1,0:T(8,128)(2,1)}, bf16[1,384,640]{2,1,0:T(8,128)(2,1)S(1)}, u32[]{:S(2)}, u32[]{:S(2)}) collective-permute-start(bf16[1,384,640]{2,1,0:T(8,128)(2,1)} %param.12), channel_id=1, source_target_pairs={{0,64},{32,96},{64,128},{96,160},{128,192},{160,224},{192,256},{22... | collective-permute-start | bytes 1474568 | tf_op jit(solution)/shard_map/ppermute | solution.py:19
  70.5 22.0 %collective-permute-start.6 = (bf16[1,384,640]{2,1,0:T(8,128)(2,1)}, bf16[1,384,640]{2,1,0:T(8,128)(2,1)S(1)}, u32[]{:S(2)}, u32[]{:S(2)}) collective-permute-start(bf16[1,384,640]{2,1,0:T(8,128)(2,1)} %param.12), channel_id=1, source_target_pairs={{0,32},{32,64},{64,96},{96,128},{128,160},{160,192},{192,224},{224... | collective-permute-start | bytes 1474568 | tf_op jit(solution)/shard_map/ppermute | solution.py:19
  72.5 2.0 copy-start.4
  72.5 20.0 %collective-permute-start.8 = (bf16[1,384,640]{2,1,0:T(8,128)(2,1)}, bf16[1,384,640]{2,1,0:T(8,128)(2,1)S(1)}, u32[]{:S(2)}, u32[]{:S(2)}) collective-permute-start(bf16[1,384,640]{2,1,0:T(8,128)(2,1)} %param.12), channel_id=1, source_target_pairs={{0,96},{32,128},{64,160},{96,192},{128,224},{160,256},{192,288},{2... | collective-permute-start | bytes 1474568 | tf_op jit(solution)/shard_map/ppermute | solution.py:19
  74.4 0.8 copy-start.5
  140.0 13.7 %copy-start.1 = (bf16[1,384,640]{2,1,0:T(8,128)(2,1)S(1)}, bf16[1,384,640]{2,1,0:T(8,128)(2,1)}, u32[]{:S(2)}) copy-start(bf16[1,384,640]{2,1,0:T(8,128)(2,1)} %param.10) | copy-start | bytes 1474564
  140.0 13.7 %copy-start.6 = (f32[640]{0:T(1024)S(1)}, f32[640]{0:T(1024)}, u32[]{:S(2)}) copy-start(f32[640]{0:T(1024)} %param.14) | copy-start | bytes 7684
  140.0 14.1 %copy-start = (f32[1,1536,640]{2,1,0:T(8,128)S(1)}, f32[1,1536,640]{2,1,0:T(8,128)}, u32[]{:S(2)}) copy-start(f32[1,1536,640]{2,1,0:T(8,128)} %get-tuple-element.163) | copy-start | bytes 11796484
  142.1 50.9 %collective-permute-start.9 = (f32[1,384,640]{2,1,0:T(8,128)S(1)}, f32[1,384,640]{2,1,0:T(8,128)S(1)}, u32[]{:S(2)}, u32[]{:S(2)}) collective-permute-start(f32[1,384,640]{2,1,0:T(8,128)S(1)} %get-tuple-element.200), channel_id=1, source_target_pairs={{32,0},{64,32},{96,64},{128,96},{160,128},{192,160},{224,192},{256... | collective-permute-start | bytes 2949128 | tf_op jit(solution)/shard_map/ppermute | solution.py:19
  149.8 64.4 %collective-permute-start.11 = (f32[1,384,640]{2,1,0:T(8,128)S(1)}, f32[1,384,640]{2,1,0:T(8,128)S(1)}, u32[]{:S(2)}, u32[]{:S(2)}) collective-permute-start(f32[1,384,640]{2,1,0:T(8,128)S(1)} %get-tuple-element.201), channel_id=1, source_target_pairs={{96,0},{128,32},{160,64},{192,96},{224,128},{256,160},{288,192},{3... | collective-permute-start | bytes 2949128 | tf_op jit(solution)/shard_map/ppermute | solution.py:19
  151.7 84.5 %collective-permute-start.10 = (f32[1,384,640]{2,1,0:T(8,128)S(1)}, f32[1,384,640]{2,1,0:T(8,128)S(1)}, u32[]{:S(2)}, u32[]{:S(2)}) collective-permute-start(f32[1,384,640]{2,1,0:T(8,128)S(1)} %get-tuple-element.202), channel_id=1, source_target_pairs={{64,0},{96,32},{128,64},{160,96},{192,128},{224,160},{256,192},{28... | collective-permute-start | bytes 2949128 | tf_op jit(solution)/shard_map/ppermute | solution.py:19
  154.0 82.2 %copy-start.2 = (bf16[1,384,640]{2,1,0:T(8,128)(2,1)S(1)}, bf16[1,384,640]{2,1,0:T(8,128)(2,1)}, u32[]{:S(2)}) copy-start(bf16[1,384,640]{2,1,0:T(8,128)(2,1)} %param.11) | copy-start | bytes 1474564
  154.1 82.2 %copy-start.7 = (f32[640]{0:T(1024)S(1)}, f32[640]{0:T(1024)}, u32[]{:S(2)}) copy-start(f32[640]{0:T(1024)} %param.15) | copy-start | bytes 7684
  155.8 294.2 %collective-permute-start.12 = (f32[1,384,640]{2,1,0:T(8,128)}, f32[1,384,640]{2,1,0:T(8,128)}, u32[]{:S(2)}, u32[]{:S(2)}) collective-permute-start(f32[1,384,640]{2,1,0:T(8,128)} %get-tuple-element.197), channel_id=1, source_target_pairs={{32,0},{64,32},{96,64},{128,96},{160,128},{192,160},{224,192},{256... | collective-permute-start | bytes 2949128 | tf_op jit(solution)/shard_map/ppermute | solution.py:19
  157.7 292.2 %collective-permute-start.14 = (f32[1,384,640]{2,1,0:T(8,128)}, f32[1,384,640]{2,1,0:T(8,128)}, u32[]{:S(2)}, u32[]{:S(2)}) collective-permute-start(f32[1,384,640]{2,1,0:T(8,128)} %get-tuple-element.198), channel_id=1, source_target_pairs={{96,0},{128,32},{160,64},{192,96},{224,128},{256,160},{288,192},{3... | collective-permute-start | bytes 2949128 | tf_op jit(solution)/shard_map/ppermute | solution.py:19
  193.0 257.0 %collective-permute-start.13 = (f32[1,384,640]{2,1,0:T(8,128)}, f32[1,384,640]{2,1,0:T(8,128)}, u32[]{:S(2)}, u32[]{:S(2)}) collective-permute-start(f32[1,384,640]{2,1,0:T(8,128)} %get-tuple-element.199), channel_id=1, source_target_pairs={{64,0},{96,32},{128,64},{160,96},{192,128},{224,160},{256,192},{28... | collective-permute-start | bytes 2949128 | tf_op jit(solution)/shard_map/ppermute | solution.py:19
where the time goes:
time: 454 us; the launch traced here: 453 us
  blocking collectives  230 us (51%)
  waiting for transfers between devices  116 us (26%)
  starting transfers between devices  38.2 us (8%)
  matrix products  34.7 us (8%)
  other arithmetic  23 us (5%)
  local copies, waits for them, and re-layouts  9.07 us (2%)
    psum x1, blocking collectives, on_device(): lax.psum((jnp.sum(q_grad * q_unit, axis=(0, 1)), jnp.sum(k_own * k_unit,...  193 us
    ppermute x15, waiting for transfers between devices, shifted(): lax.ppermute(value, axis, [(source, source + steps) for source in range(l...  116 us
    ppermute x15, starting transfers between devices, shifted(): lax.ppermute(value, axis, [(source, source + steps) for source in range(l...  38.2 us
    psum x1, blocking collectives, on_device(): lax.psum((jnp.sum(q_wide * q_wide, axis=-1), jnp.sum(k_wide * k_wide, axi...  20.2 us
    psum x1, blocking collectives, on_device(): lax.psum((jnp.sum(q_scaled * q_unit, axis=-1), jnp.sum(k_scaled * k_unit,...  16.8 us
    dot_general x5, matrix products, query_head(): jnp.einsum('rqk,rqd->rkd', weights.astype(jnp.bfloat16), g_head, preferre...  13.2 us
  transfers between devices with their start and end apart: 15, of which 5 were waited for; matrix products, arithmetic and copies ran while one was open for 3% of the time, Pallas kernels for 0%

commit v1 on v0

v1 whole, which is shorter than its diff:
```python
import functools
import math

import jax
import jax.numpy as jnp
from jax import lax
from jax.experimental import pallas as pl
from jax.experimental.pallas import tpu as pltpu
from jax.sharding import PartitionSpec as P

HD = 128
EPSILON = 1e-06
MASKED = -1e30
CHUNKS = ((0, 2), (2, 5))
STRIP = 48
F32, LOW = jnp.float32, jnp.bfloat16
VMEM_LIMIT = 60 * 1024 * 1024


def along_lanes(row, width):
    return jnp.transpose(jnp.broadcast_to(row, (width, row.shape[1])))


def row_sums(block):
    return jnp.sum(jnp.transpose(block), axis=0, keepdims=True)


def folded(block, op):
    return functools.reduce(op, [block[at : at + 8] for at in range(0, block.shape[0], 8)])


def prepare_kernel(q_ref, k_ref, v_ref, own_out, power_out, total):
    slots = q_ref.shape[1]
    own_out[:slots, :] = k_ref[0]
    own_out[slots:, :] = v_ref[0]

    @pl.when(pl.program_id(0) == 0)
    def _():
        total[...] = jnp.zeros_like(total)

    for place, ref in enumerate((q_ref, k_ref)):
        part = ref[0].astype(F32)
        total[place] += part * part

    @pl.when(pl.program_id(0) == pl.num_programs(0) - 1)
    def _():
        for place in range(2):
            row = row_sums(total[place])
            for device in range(power_out.shape[0]):
                power_out[device, :, place * slots : (place + 1) * slots] = row


def roots_kernel(full_width, tag_ref, power_ref, note_out, q_out):
    slots = q_out.shape[1]
    power = power_ref[0]
    for device in range(1, power_ref.shape[0]):
        power += power_ref[device]
    inverse = 1.0 / jnp.sqrt(power / full_width + EPSILON)
    q_out[...] = inverse[:, :slots]
    lane = lax.broadcasted_iota(jnp.int32, (1, HD), 1)
    valid = tag_ref[1].astype(F32)
    segment = tag_ref[2].astype(F32)
    tags = jnp.where(lane == 0, valid, jnp.where(lane == 1, segment, 0.0))
    for device in range(note_out.shape[0]):
        note_out[device, :, :slots] = inverse[:, slots:]
        note_out[device, :, slots:] = tags


def head_kernel(
    first, total_heads, tag_ref, notes, q_inverse, gain_q_ref, gain_k_ref, q_ref, g_ref,
    own_ref, near_ref, side_ref, swap_ref, state_in,
    q_out, own_out, near_out, side_out, swap_out, state_out, rows_out,
    score_ref, grad_ref, weight_low, grad_low,
):
    step = pl.program_id(0)
    slots = q_ref.shape[1]
    width = total_heads * HD
    scale = 1.0 / math.sqrt(HD)
    mine = tag_ref[0]
    even = lax.rem(mine, 2) == 0
    distances = (0, 2, jnp.where(even, 3, 1), jnp.where(even, 1, 3))
    gain_q = gain_q_ref[...]
    gain_k = gain_k_ref[...]
    segment = tag_ref[2].astype(F32)
    q_unit = q_ref[0].astype(F32) * along_lanes(q_inverse[...], HD)
    q_norm = (q_unit * gain_q).astype(LOW)
    live = lax.broadcasted_iota(jnp.int32, (slots, HD), 0) < tag_ref[1]
    g_live = jnp.where(live, g_ref[0].astype(F32), 0.0).astype(LOW)
    q_side = jnp.transpose(q_norm)
    g_side = jnp.transpose(g_live)
    lanes = lax.broadcasted_iota(jnp.int32, (STRIP, slots), 0).astype(F32)
    refs = (own_ref, near_ref, side_ref, swap_ref)
    inverses, k_norms, limits = [], [], []
    for slot, ref in enumerate(refs):
        other = mine - distances[slot]
        at = jnp.maximum(other, 0)
        inverse = along_lanes(notes[at, :, :slots], HD)
        tags = notes[at, :, slots:]
        same = (tags[:, 1:2] == segment) & (other >= 0)
        limits.append(jnp.where(same, tags[:, 0:1], 0.0))
        k_norm = (ref[:slots, :].astype(F32) * inverse * gain_k).astype(LOW)
        inverses.append(inverse)
        k_norms.append(k_norm)
        rows = slice(slot * slots, (slot + 1) * slots)
        score_ref[rows, :] = jnp.dot(k_norm, q_side, preferred_element_type=F32)
        grad_ref[rows, :] = jnp.dot(ref[slots:, :], g_side, preferred_element_type=F32)
    strips = [(slot, at) for slot in range(4) for at in range(0, slots, STRIP)]
    top = jnp.full((8, slots), MASKED, F32)
    for slot, at in strips:
        base = slot * slots + at
        included = lanes < limits[slot] - at
        score = jnp.where(included, score_ref[base : base + STRIP, :], MASKED)
        top = jnp.maximum(top, folded(score, jnp.maximum))
    top = jnp.max(top, axis=0, keepdims=True)
    total = jnp.zeros((8, slots), F32)
    delta = jnp.zeros((8, slots), F32)
    for slot, at in strips:
        base = slot * slots + at
        included = lanes < limits[slot] - at
        score = jnp.where(included, score_ref[base : base + STRIP, :], MASKED)
        exponent = jnp.exp((score - top) * scale)
        score_ref[base : base + STRIP, :] = exponent
        total += folded(exponent, jnp.add)
        delta += folded(exponent * grad_ref[base : base + STRIP, :], jnp.add)
    inverse_sum = 1.0 / jnp.sum(total, axis=0, keepdims=True)
    delta = jnp.sum(delta, axis=0, keepdims=True) * inverse_sum
    q_turned = jnp.zeros((HD, slots), F32)
    k_gain = jnp.zeros((1, HD), F32)
    inners = []
    for slot, out in enumerate((own_out, near_out, side_out, swap_out)):
        for at in range(0, slots, STRIP):
            rows = slice(slot * slots + at, slot * slots + at + STRIP)
            weight = score_ref[rows, :] * inverse_sum
            weight_low[rows, :] = weight.astype(LOW)
            grad_low[rows, :] = (weight * (grad_ref[rows, :] - delta)).astype(LOW)
        rows = slice(slot * slots, (slot + 1) * slots)
        q_turned += jnp.dot(
            jnp.transpose(k_norms[slot]), grad_low[rows, :], preferred_element_type=F32
        )
        k_part = jnp.dot(grad_low[rows, :], q_norm, preferred_element_type=F32) * scale
        v_part = jnp.dot(weight_low[rows, :], g_live, preferred_element_type=F32)
        out[:slots, :] = k_part.astype(out.dtype)
        out[slots:, :] = v_part.astype(out.dtype)
        product = k_part * (refs[slot][:slots, :].astype(F32) * inverses[slot])
        k_gain += jnp.sum(product, axis=0, keepdims=True)
        inners.append(row_sums(product * gain_k))
    q_part = jnp.transpose(q_turned) * scale
    q_out[...] = q_part
    product = q_part * q_unit
    inners.append(row_sums(product * gain_q))

    @pl.when(step == 0)
    def _():
        state_out[...] = state_in[...]

    for slot, inner in enumerate(inners):
        state_out[slot : slot + 1, :slots] += inner
    at = (first + step) * HD
    state_out[5:6, pl.ds(pl.multiple_of(at, HD), HD)] = jnp.sum(product, axis=0, keepdims=True)
    state_out[5:6, pl.ds(pl.multiple_of(width + at, HD), HD)] = k_gain

    @pl.when(first + step == total_heads - 1)
    def _():
        for device in range(rows_out.shape[0]):
            rows_out[device, :, :slots] = jnp.zeros((1, slots), F32)
            rows_out[device, :, slots:] = state_out[5:6, :]
        for slot, distance in enumerate(distances):
            @pl.when(mine >= distance)
            def _():
                rows_out[mine - distance, :, :slots] = state_out[slot : slot + 1, :slots]


def collect_kernel(state_ref, rows_ref, out):
    slots = rows_ref.shape[2] - state_ref.shape[1]
    total = rows_ref[0]
    for device in range(1, rows_ref.shape[0]):
        total += rows_ref[device]
    for device in range(out.shape[0]):
        out[device, :, :slots] = state_ref[4:5, :slots]
        out[device, :, slots:] = total


def finish_kernel(
    full_width, sizes, tag_ref, notes, q_inverse, gain_q_ref, gain_k_ref, sums, q_ref, k_ref,
    q_part, own_part, side_back, near_back, *rest,
):
    query_out, key_out, value_out, gain_out = rest[-4:]
    slots = q_ref.shape[1]
    mine, mp, dp = tag_ref[0], tag_ref[3], tag_ref[4]
    mp_size, dp_size = sizes
    inner = sums[dp, :, : 2 * slots]
    for other in range(1, mp_size):
        inner += sums[other * dp_size + dp, :, : 2 * slots]
    inner = inner / full_width

    @pl.when(pl.program_id(0) == 0)
    def _():
        gain = sums[mp * dp_size, :, 2 * slots :]
        for other in range(1, dp_size):
            gain += sums[mp * dp_size + other, :, 2 * slots :]
        gain_out[...] = gain

    inverse = along_lanes(q_inverse[...], HD)
    unit = q_ref[0].astype(F32) * inverse
    scaled = q_part[...] * gain_q_ref[...]
    query_out[0] = ((scaled - unit * along_lanes(inner[:, :slots], HD)) * inverse).astype(LOW)
    inverse = along_lanes(notes[mine, :, :slots], HD)
    unit = k_ref[0].astype(F32) * inverse
    keep = jnp.where(lax.rem(mine, 2) == 0, 1.0, 0.0)
    total = own_part[...] + near_back[...].astype(F32) + side_back[...].astype(F32) * keep
    scaled = total[:slots] * gain_k_ref[...]
    key_out[0] = ((scaled - unit * along_lanes(inner[:, slots:], HD)) * inverse).astype(LOW)
    value_out[0] = total[slots:].astype(LOW)


def struct(shape, dtype=F32):
    return jax.ShapeDtypeStruct(shape, dtype)


def kernel_params():
    return pltpu.CompilerParams(vmem_limit_bytes=VMEM_LIMIT)


def on_device(q_proj, k_proj, values, grad_out, gain_q, gain_k, valid_count, segment):
    _, slots, local_width = q_proj.shape
    heads = local_width // HD
    mp_size, dp_size = lax.axis_size("mp"), lax.axis_size("dp")
    full_width = local_width * mp_size
    groups = lax.axis_size("tm")
    mine = lax.axis_index("tm")
    even = mine % 2 == 0
    tags = jnp.stack(
        [mine, valid_count[0, 0], segment[0, 0], lax.axis_index("mp"), lax.axis_index("dp")]
    ).astype(jnp.int32)
    gain_q = gain_q.reshape(1, local_width)
    gain_k = gain_k.reshape(1, local_width)
    smem = pl.BlockSpec(memory_space=pltpu.SMEM)

    two_on = [(i, i + 2) for i in range(groups - 2)]
    one_on = [(i, i + 1) for i in range(groups - 1)]
    pair = [(i, i ^ 1) for i in range(groups)]
    back = lambda moves: [(there, here) for here, there in moves]

    def head_blocks(first, rows):
        return pl.BlockSpec((rows, HD), lambda head: (0, first + head))

    def raw_blocks(first):
        return pl.BlockSpec((1, slots, HD), lambda head: (0, 0, first + head))

    def all_of(shape):
        return pl.BlockSpec(shape, lambda head: (0,) * len(shape))

    own, power = pl.pallas_call(
        prepare_kernel,
        grid=(heads,),
        in_specs=[raw_blocks(0)] * 3,
        out_specs=[head_blocks(0, 2 * slots), all_of((mp_size, 1, 2 * slots))],
        out_shape=[struct((2 * slots, local_width), LOW), struct((mp_size, 1, 2 * slots))],
        scratch_shapes=[pltpu.VMEM((2, slots, HD), F32)],
        compiler_params=kernel_params(),
        cost_estimate=pl.CostEstimate(flops=10**6, bytes_accessed=3 * 10**6, transcendentals=0),
    )(q_proj, k_proj, values)
    near = lax.ppermute(own, "tm", two_on)
    powers = lax.all_to_all(power, "mp", 0, 0, tiled=True)
    note, q_inverse = pl.pallas_call(
        functools.partial(roots_kernel, full_width),
        in_specs=[smem, pl.BlockSpec()],
        out_shape=[struct((groups, 1, slots + HD)), struct((1, slots))],
        compiler_params=kernel_params(),
    )(tags, powers)
    notes = lax.all_to_all(note, "tm", 0, 0, tiled=True)
    near, notes = lax.optimization_barrier((near, notes))
    side = lax.ppermute(jnp.where(even, own, near), "tm", one_on)
    swap = lax.ppermute(near, "tm", pair)

    state = jnp.zeros((8, 2 * local_width), F32)
    parts = []
    for first, last in CHUNKS:
        width = (last - first) * HD
        row_shape = (groups, 1, slots + 2 * local_width)
        q_part, own_part, near_part, side_part, swap_part, state, rows = pl.pallas_call(
            functools.partial(head_kernel, first, heads),
            grid=(last - first,),
            in_specs=[
                smem,
                all_of(notes.shape),
                all_of((1, slots)),
                head_blocks(first, 1),
                head_blocks(first, 1),
                raw_blocks(first),
                raw_blocks(first),
                *[head_blocks(first, 2 * slots)] * 4,
                all_of(state.shape),
            ],
            out_specs=[
                head_blocks(0, slots),
                *[head_blocks(0, 2 * slots)] * 4,
                all_of(state.shape),
                all_of(row_shape),
            ],
            out_shape=[
                struct((slots, width)),
                struct((2 * slots, width)),
                *[struct((2 * slots, width), LOW)] * 3,
                struct(state.shape),
                struct(row_shape),
            ],
            scratch_shapes=[
                pltpu.VMEM((4 * slots, slots), F32),
                pltpu.VMEM((4 * slots, slots), F32),
                pltpu.VMEM((4 * slots, slots), LOW),
                pltpu.VMEM((4 * slots, slots), LOW),
            ],
            compiler_params=kernel_params(),
            cost_estimate=pl.CostEstimate(
                flops=(last - first) * 40 * slots * slots * HD,
                bytes_accessed=(last - first) * 44 * slots * HD,
                transcendentals=(last - first) * 4 * slots * slots,
            ),
        )(tags, notes, q_inverse, gain_q, gain_k, q_proj, grad_out, own, near, side, swap, state)
        side_back = lax.ppermute(side_part, "tm", back(one_on))
        swap_back = lax.ppermute(swap_part, "tm", pair)
        near_sum = near_part.astype(F32) + swap_back.astype(F32)
        near_sum = near_sum + jnp.where(even, 0.0, side_back.astype(F32))
        near_sum = near_sum.astype(LOW)
        if last < heads:
            near_back = lax.ppermute(near_sum, "tm", back(two_on))
            early = near_sum
        else:
            rows, early = lax.optimization_barrier((rows, early))
            rows = lax.all_to_all(rows, "tm", 0, 0, tiled=True)
            rows, near_sum = lax.optimization_barrier((rows, near_sum))
            near_back = lax.ppermute(near_sum, "tm", back(two_on))
        parts.append((q_part, own_part, side_back, near_back))

    sums = pl.pallas_call(
        collect_kernel,
        out_shape=struct((mp_size * dp_size, 1, 2 * slots + 2 * local_width)),
        compiler_params=kernel_params(),
    )(state, rows)
    sums = lax.all_to_all(sums, ("mp", "dp"), 0, 0, tiled=True)

    outs = ()
    for (first, last), part in zip(CHUNKS, parts):
        specs = [
            smem,
            all_of(notes.shape),
            all_of((1, slots)),
            head_blocks(first, 1),
            head_blocks(first, 1),
            all_of(sums.shape),
            raw_blocks(first),
            raw_blocks(first),
            head_blocks(0, slots),
            *[head_blocks(0, 2 * slots)] * 3,
        ]
        *outs, gain = pl.pallas_call(
            functools.partial(finish_kernel, full_width, (mp_size, dp_size)),
            grid=(last - first,),
            in_specs=specs + [pl.BlockSpec(memory_space=pl.ANY)] * len(outs),
            out_specs=[*[raw_blocks(first)] * 3, all_of((1, 2 * local_width))],
            out_shape=[*[struct(q_proj.shape, LOW)] * 3, struct((1, 2 * local_width))],
            input_output_aliases={len(specs) + i: i for i in range(len(outs))},
            compiler_params=kernel_params(),
            cost_estimate=pl.CostEstimate(flops=10**6, bytes_accessed=5 * 10**6, transcendentals=0),
        )(tags, notes, q_inverse, gain_q, gain_k, sums, q_proj, k_proj, *part, *outs)
    return (*outs, gain[0, :local_width], gain[0, local_width:])


def solution(mesh):
    wide = P("dp", "tm", "mp")
    in_specs = (wide, wide, wide, wide, P("mp"), P("mp"), P("dp", "tm"), P("dp", "tm"))
    out_specs = (wide, wide, wide, P("mp"), P("mp"))
    return jax.shard_map(
        on_device, mesh=mesh, in_specs=in_specs, out_specs=out_specs, check_vma=False
    )
```

time: 454 us -> 146 us (0.32)
  the two profiles are of different devices: /device:TPU:72 before, /device:TPU:6 now
where the time goes in v1:
time: 146 us; the launch traced here: 145 us
  starting transfers between devices  57.7 us (40%)
  waiting for transfers between devices  38.5 us (26%)
  Pallas kernels  36.6 us (25%)
  local copies, waits for them, and re-layouts  7.6 us (5%)
  between operations  2.21 us (2%)
  other arithmetic  2.11 us (1%)
    pallas_call x2, Pallas kernels, on_device(): pl.pallas_call(functools.partial(head_kernel, first, heads), grid=(last -...  21.8 us
    ppermute x2, waiting for transfers between devices, on_device(): near_back = lax.ppermute(near_sum, 'tm', back(two_on))  16.6 us
    all_to_all x1, starting transfers between devices, on_device(): powers = lax.all_to_all(power, 'mp', 0, 0, tiled=True)  10.3 us
    all_to_all x1, starting transfers between devices, on_device(): sums = lax.all_to_all(sums, ('mp', 'dp'), 0, 0, tiled=True)  9.46 us
    ppermute x1, waiting for transfers between devices, on_device(): side = lax.ppermute(jnp.where(even, own, near), 'tm', one_on)  8.26 us
    all_to_all x1, starting transfers between devices, on_device(): rows = lax.all_to_all(rows, 'tm', 0, 0, tiled=True)  7.56 us
    pallas_call x2, Pallas kernels, on_device(): pl.pallas_call(functools.partial(finish_kernel, full_width, (mp_size, dp_...  7.36 us
    ppermute x2, starting transfers between devices, on_device(): side_back = lax.ppermute(side_part, 'tm', back(one_on))  5.97 us
  transfers between devices with their start and end apart: 13, of which 5 were waited for; matrix products, arithmetic and copies ran while one was open for 2% of the time, Pallas kernels for 13%

profile of v1, /device:TPU:6, one launch (start us, length us, event | category | flops | bytes accessed | tf_op | source)
XLA Modules:
  0.0 144.7 jit_solution(1977702327589330273)
XLA Ops:
  0.6 4.3 %shard_map.119 = (bf16[768,640]{1,0:T(8,128)(2,1)}, f32[8,1,768]{2,1,0:T(1,128)}) custom-call(bf16[1,384,640]{2,1,0:T(8,128)(2,1)} %q_ref.9, bf16[1,384,640]{2,1,0:T(8,128)(2,1)} %k_ref.5, bf16[1,384,640]{2,1,0:T(8,128)(2,1)} %v_ref.1), custom_call_target="tpu_custom_call" | custom-call | flops 1000000 | bytes 3000000 | tf_op jit(solution)/shard_map/pallas_call | solution.py:253
  5.0 3.4 %collective-permute-start = (bf16[768,640]{1,0:T(8,128)(2,1)}, bf16[768,640]{1,0:T(8,128)(2,1)S(1)}, u32[]{:S(2)}, u32[]{:S(2)}) collective-permute-start(bf16[768,640]{1,0:T(8,128)(2,1)} %get-tuple-element.34.own_ref), channel_id=1, source_target_pairs={{0,64},{32,96},{64,128},{96,160},{128,192},{160,224},{192,256},{22... | collective-permute-start | bytes 2949128 | tf_op jit(solution)/shard_map/ppermute | solution.py:263
  8.4 10.3 %all-to-all-start = ((f32[8,1,768]{2,1,0:T(1,128)}), f32[8,1,768]{2,1,0:T(1,128)S(1)}, u32[]{:S(2)}, u32[]{:S(2)}) async-start(f32[8,1,768]{2,1,0:T(1,128)} %get-tuple-element.35), calls=%async_computation | async-start | bytes 49152 | tf_op jit(solution)/shard_map/all_to_all | solution.py:264
  20.0 0.7 stack.15.tag_ref
  20.7 5.9 %all-to-all-done.power_ref = f32[8,1,768]{2,1,0:T(1,128)S(1)} async-done(((f32[8,1,768]{2,1,0:T(1,128)}), f32[8,1,768]{2,1,0:T(1,128)S(1)}, u32[]{:S(2)}, u32[]{:S(2)}) %all-to-all-start) | async-done | bytes 24608 | tf_op jit(solution)/shard_map/all_to_all | solution.py:264
  26.5 0.6 copy-done.10
  27.1 1.4 shard_map.120
  28.5 5.5 %all-to-all-start.1 = ((f32[16,1,512]{2,1,0:T(1,128)}), f32[16,1,512]{2,1,0:T(1,128)S(1)}, u32[]{:S(2)}, u32[]{:S(2)}) async-start(f32[16,1,512]{2,1,0:T(1,128)} %get-tuple-element.36), calls=%async_computation.1 | async-start | bytes 65536 | tf_op jit(solution)/shard_map/all_to_all | solution.py:271
  34.0 0.0 copy-start.12
  34.0 4.2 %all-to-all-done.1.notes = f32[16,1,512]{2,1,0:T(1,128)S(1)} async-done(((f32[16,1,512]{2,1,0:T(1,128)}), f32[16,1,512]{2,1,0:T(1,128)S(1)}, u32[]{:S(2)}, u32[]{:S(2)}) %all-to-all-start.1) | async-done | bytes 32800 | tf_op jit(solution)/shard_map/all_to_all | solution.py:271
  38.2 0.0 collective-permute-done.near_ref
  38.2 1.7 %broadcast_select_fusion = bf16[768,640]{1,0:T(8,128)(2,1)S(1)} fusion(bf16[768,640]{1,0:T(8,128)(2,1)} %get-tuple-element.34.own_ref, bf16[768,640]{1,0:T(8,128)(2,1)S(1)} %collective-permute-done.near_ref, pred[]{:T(512)S(6)} %eq.5), kind=kLoop, calls=%fused_computation.1 | loop fusion | flops 491520 | bytes 2949121 | tf_op jit(solution)/shard_map/jit(_where)/select_n | solution.py:273
  39.9 1.9 %collective-permute-start.1 = (bf16[768,640]{1,0:T(8,128)(2,1)S(1)}, bf16[768,640]{1,0:T(8,128)(2,1)S(1)}, u32[]{:S(2)}, u32[]{:S(2)}) collective-permute-start(bf16[768,640]{1,0:T(8,128)(2,1)S(1)} %broadcast_select_fusion), channel_id=1, source_target_pairs={{0,32},{32,64},{64,96},{96,128},{128,160},{160,192},{192,224},{224... | collective-permute-start | bytes 2949128 | tf_op jit(solution)/shard_map/ppermute | solution.py:273
  41.9 4.0 %collective-permute-start.2 = (bf16[768,640]{1,0:T(8,128)(2,1)S(1)}, bf16[768,640]{1,0:T(8,128)(2,1)S(1)}, u32[]{:S(2)}, u32[]{:S(2)}) collective-permute-start(bf16[768,640]{1,0:T(8,128)(2,1)S(1)} %collective-permute-done.near_ref), channel_id=1, source_target_pairs={{0,32},{32,0},{64,96},{96,64},{128,160},{160,128},{192,224},{224,1... | collective-permute-start | bytes 2949128 | tf_op jit(solution)/shard_map/ppermute | solution.py:274
  45.9 0.6 reshape.16.gain_q_ref
  46.5 0.6 reshape.17.gain_k_ref
  47.1 8.3 %collective-permute-done.1.side_ref = bf16[768,640]{1,0:T(8,128)(2,1)S(1)} collective-permute-done((bf16[768,640]{1,0:T(8,128)(2,1)S(1)}, bf16[768,640]{1,0:T(8,128)(2,1)S(1)}, u32[]{:S(2)}, u32[]{:S(2)}) %collective-permute-start.1) | collective-permute-done | bytes 983072 | tf_op jit(solution)/shard_map/ppermute | solution.py:273
  55.3 0.0 collective-permute-done.2.swap_ref
  55.3 1.0 copy-done.14
  56.4 0.6 broadcast_in_dim.11.state_in
  57.0 9.1 %shard_map.121 = (f32[384,256]{1,0:T(8,128)}, f32[768,256]{1,0:T(8,128)}, bf16[768,256]{1,0:T(8,128)(2,1)}, bf16[768,256]{1,0:T(8,128)(2,1)}, bf16[768,256]{1,0:...) custom-call(s32[5]{0:T(128)} %stack.15.tag_ref, f32[16,1,512]{2,1,0:T(1,128)} %copy-done.9, ...), custom_call_target="tpu_custom_call" | custom-call | flops 1509949440 | bytes 4325376 | tf_op jit(solution)/shard_map/pallas_call | solution.py:281
  66.1 1.9 %collective-permute-start.3 = (bf16[768,256]{1,0:T(8,128)(2,1)}, bf16[768,256]{1,0:T(8,128)(2,1)S(1)}, u32[]{:S(2)}, u32[]{:S(2)}) collective-permute-start(bf16[768,256]{1,0:T(8,128)(2,1)} %get-tuple-element.44), channel_id=1, source_target_pairs={{0,32},{32,0},{64,96},{96,64},{128,160},{160,128},{192,224},{224,1... | collective-permute-start | bytes 1179656 | tf_op jit(solution)/shard_map/ppermute | solution.py:322
  68.0 2.5 %collective-permute-start.4 = (bf16[768,256]{1,0:T(8,128)(2,1)}, bf16[768,256]{1,0:T(8,128)(2,1)S(1)}, u32[]{:S(2)}, u32[]{:S(2)}) collective-permute-start(bf16[768,256]{1,0:T(8,128)(2,1)} %get-tuple-element.45), channel_id=1, source_target_pairs={{32,0},{64,32},{96,64},{128,96},{160,128},{192,160},{224,192},{256... | collective-permute-start | bytes 1179656 | tf_op jit(solution)/shard_map/ppermute | solution.py:321
  70.5 0.0 copy-start.7
  70.6 12.7 %shard_map.122 = (f32[384,384]{1,0:T(8,128)}, f32[768,384]{1,0:T(8,128)}, bf16[768,384]{1,0:T(8,128)(2,1)}, bf16[768,384]{1,0:T(8,128)(2,1)}, bf16[768,384]{1,0:...) custom-call(s32[5]{0:T(128)} %stack.15.tag_ref, f32[16,1,512]{2,1,0:T(1,128)} %copy-done.9, ...), custom_call_target="tpu_custom_call" | custom-call | flops 2264924160 | bytes 6488064 | tf_op jit(solution)/shard_map/pallas_call | solution.py:281
  83.3 2.1 %collective-permute-start.5 = (bf16[768,384]{1,0:T(8,128)(2,1)}, bf16[768,384]{1,0:T(8,128)(2,1)S(1)}, u32[]{:S(2)}, u32[]{:S(2)}) collective-permute-start(bf16[768,384]{1,0:T(8,128)(2,1)} %get-tuple-element.48), channel_id=1, source_target_pairs={{0,32},{32,0},{64,96},{96,64},{128,160},{160,128},{192,224},{224,1... | collective-permute-start | bytes 1769480 | tf_op jit(solution)/shard_map/ppermute | solution.py:322
  85.3 3.5 %collective-permute-start.6 = (bf16[768,384]{1,0:T(8,128)(2,1)}, bf16[768,384]{1,0:T(8,128)(2,1)S(1)}, u32[]{:S(2)}, u32[]{:S(2)}) collective-permute-start(bf16[768,384]{1,0:T(8,128)(2,1)} %get-tuple-element.49), channel_id=1, source_target_pairs={{32,0},{64,32},{96,64},{128,96},{160,128},{192,160},{224,192},{256... | collective-permute-start | bytes 1769480 | tf_op jit(solution)/shard_map/ppermute | solution.py:321
  88.8 0.0 collective-permute-done.3
  88.8 0.0 collective-permute-done.4.side_back
  88.8 0.2 add_convert_fusion.1
  89.0 7.6 %all-to-all-start.2 = ((f32[16,1,1664]{2,1,0:T(1,128)}), f32[16,1,1664]{2,1,0:T(1,128)S(1)}, u32[]{:S(2)}, u32[]{:S(2)}) async-start(f32[16,1,1664]{2,1,0:T(1,128)} %get-tuple-element.46), calls=%async_computation.2 | async-start | bytes 212992 | tf_op jit(solution)/shard_map/all_to_all | solution.py:331
  96.6 0.0 collective-permute-done.5
  96.6 0.0 collective-permute-done.6.side_back
  96.6 0.3 add_convert_fusion
  96.9 0.5 copy-done
  97.4 3.6 %all-to-all-done.2.rows_ref = f32[16,1,1664]{2,1,0:T(1,128)S(1)} async-done(((f32[16,1,1664]{2,1,0:T(1,128)}), f32[16,1,1664]{2,1,0:T(1,128)S(1)}, u32[]{:S(2)}, u32[]{:S(2)}) %all-to-all-start.2) | async-done | bytes 106528 | tf_op jit(solution)/shard_map/all_to_all | solution.py:331
  101.0 2.3 %collective-permute-start.7 = (bf16[768,384]{1,0:T(8,128)(2,1)S(1)}, bf16[768,384]{1,0:T(8,128)(2,1)S(1)}, u32[]{:S(2)}, u32[]{:S(2)}) collective-permute-start(bf16[768,384]{1,0:T(8,128)(2,1)S(1)} %add_convert_fusion), channel_id=1, source_target_pairs={{64,0},{96,32},{128,64},{160,96},{192,128},{224,160},{256,192},{28... | collective-permute-start | bytes 1769480 | tf_op jit(solution)/shard_map/ppermute | solution.py:333
  103.3 1.7 %shard_map.123 = f32[32,1,2048]{2,1,0:T(1,128)} custom-call(f32[8,1280]{1,0:T(8,128)} %get-tuple-element.41.state_ref, f32[16,1,1664]{2,1,0:T(1,128)} %copy-done.6), custom_call_target="tpu_custom_call" | custom-call | tf_op jit(solution)/shard_map/pallas_call | solution.py:336
  105.0 9.5 %all-to-all-start.3 = ((f32[32,1,2048]{2,1,0:T(1,128)}), f32[32,1,2048]{2,1,0:T(1,128)S(1)}, u32[]{:S(2)}, u32[]{:S(2)}) async-start(f32[32,1,2048]{2,1,0:T(1,128)} %shard_map.123), calls=%async_computation.3 | async-start | bytes 524288 | tf_op jit(solution)/shard_map/all_to_all | solution.py:341
  114.5 3.3 %collective-permute-start.8 = (bf16[768,256]{1,0:T(8,128)(2,1)S(1)}, bf16[768,256]{1,0:T(8,128)(2,1)S(1)}, u32[]{:S(2)}, u32[]{:S(2)}) collective-permute-start(bf16[768,256]{1,0:T(8,128)(2,1)S(1)} %add_convert_fusion.1), channel_id=1, source_target_pairs={{64,0},{96,32},{128,64},{160,96},{192,128},{224,160},{256,192},{28... | collective-permute-start | bytes 1179656 | tf_op jit(solution)/shard_map/ppermute | solution.py:327
  117.7 16.6 %collective-permute-done.8.near_back = bf16[768,256]{1,0:T(8,128)(2,1)S(1)} collective-permute-done((bf16[768,256]{1,0:T(8,128)(2,1)S(1)}, bf16[768,256]{1,0:T(8,128)(2,1)S(1)}, u32[]{:S(2)}, u32[]{:S(2)}) %collective-permute-start.8) | collective-permute-done | bytes 393248 | tf_op jit(solution)/shard_map/ppermute | solution.py:327
  134.4 0.0 all-to-all-done.3.sums
  134.4 0.8 copy-done.8
  135.1 0.1 copy-done.1
  135.2 3.0 %shard_map.124 = (bf16[1,384,640]{2,1,0:T(8,128)(2,1)}, bf16[1,384,640]{2,1,0:T(8,128)(2,1)}, bf16[1,384,640]{2,1,0:T(8,128)(2,1)}, f32[1,1280]{1,0:T(1,128)}) custom-call(s32[5]{0:T(128)} %stack.15.tag_ref, f32[16,1,512]{2,1,0:T(1,128)} %copy-done.9, f32[1,384]{1,0:T(1,128)} %get-tuple-element.38.q_inverse, f32[1,640]{1,0:T(1,128)} %reshape.16.gain_q_ref, ...), custom_call_target="tpu_custom_call" | custom-call | flops 1000000 | bytes 5000000 | tf_op jit(solution)/shard_map/pallas_call | solution.py:357
  138.2 0.8 copy-done.4
  139.0 4.4 %shard_map.125 = (bf16[1,384,640]{2,1,0:T(8,128)(2,1)}, bf16[1,384,640]{2,1,0:T(8,128)(2,1)}, bf16[1,384,640]{2,1,0:T(8,128)(2,1)}, f32[1,1280]{1,0:T(1,128)}) custom-call(s32[5]{0:T(128)} %stack.15.tag_ref, f32[16,1,512]{2,1,0:T(1,128)} %copy-done.9, ...), custom_call_target="tpu_custom_call", output_to_operand_aliasing={{0}: (12, {}), {1}: (13, {}), {2}: (14, {})} | custom-call | flops 1000000 | bytes 5000000 | tf_op jit(solution)/shard_map/pallas_call | solution.py:357
  143.4 1.3 slice_reduce_fusion
  (23 shorter events, 0.0 us)
Async XLA Ops:
  5.0 33.3 %collective-permute-start = (bf16[768,640]{1,0:T(8,128)(2,1)}, bf16[768,640]{1,0:T(8,128)(2,1)S(1)}, u32[]{:S(2)}, u32[]{:S(2)}) collective-permute-start(bf16[768,640]{1,0:T(8,128)(2,1)} %get-tuple-element.34.own_ref), channel_id=1, source_target_pairs={{0,64},{32,96},{64,128},{96,160},{128,192},{160,224},{192,256},{22... | collective-permute-start | bytes 2949128 | tf_op jit(solution)/shard_map/ppermute | solution.py:263
  8.4 18.1 %all-to-all-start = ((f32[8,1,768]{2,1,0:T(1,128)}), f32[8,1,768]{2,1,0:T(1,128)S(1)}, u32[]{:S(2)}, u32[]{:S(2)}) async-start(f32[8,1,768]{2,1,0:T(1,128)} %get-tuple-element.35), calls=%async_computation | async-start | bytes 49152 | tf_op jit(solution)/shard_map/all_to_all | solution.py:264
  26.5 0.6 copy-start.10
  28.5 9.7 %all-to-all-start.1 = ((f32[16,1,512]{2,1,0:T(1,128)}), f32[16,1,512]{2,1,0:T(1,128)S(1)}, u32[]{:S(2)}, u32[]{:S(2)}) async-start(f32[16,1,512]{2,1,0:T(1,128)} %get-tuple-element.36), calls=%async_computation.1 | async-start | bytes 65536 | tf_op jit(solution)/shard_map/all_to_all | solution.py:271
  34.0 11.9 %copy-start.11 = (f32[640]{0:T(1024)S(1)}, f32[640]{0:T(1024)}, u32[]{:S(2)}) copy-start(f32[640]{0:T(1024)} %param.12) | copy-start | bytes 7684
  34.0 12.5 %copy-start.12 = (f32[640]{0:T(1024)S(1)}, f32[640]{0:T(1024)}, u32[]{:S(2)}) copy-start(f32[640]{0:T(1024)} %param.13) | copy-start | bytes 7684
  38.2 1.7 %copy-start.9 = (f32[16,1,512]{2,1,0:T(1,128)}, f32[16,1,512]{2,1,0:T(1,128)S(1)}, u32[]{:S(2)}) copy-start(f32[16,1,512]{2,1,0:T(1,128)S(1)} %all-to-all-done.1.notes) | copy-start | bytes 98308
  38.2 3.6 %copy-start.3 = (bf16[768,640]{1,0:T(8,128)(2,1)}, bf16[768,640]{1,0:T(8,128)(2,1)S(1)}, u32[]{:S(2)}) copy-start(bf16[768,640]{1,0:T(8,128)(2,1)S(1)} %collective-permute-done.near_ref) | copy-start | bytes 2949124
  39.9 15.4 %collective-permute-start.1 = (bf16[768,640]{1,0:T(8,128)(2,1)S(1)}, bf16[768,640]{1,0:T(8,128)(2,1)S(1)}, u32[]{:S(2)}, u32[]{:S(2)}) collective-permute-start(bf16[768,640]{1,0:T(8,128)(2,1)S(1)} %broadcast_select_fusion), channel_id=1, source_target_pairs={{0,32},{32,64},{64,96},{96,128},{128,160},{160,192},{192,224},{224... | collective-permute-start | bytes 2949128 | tf_op jit(solution)/shard_map/ppermute | solution.py:273
  41.9 13.5 %collective-permute-start.2 = (bf16[768,640]{1,0:T(8,128)(2,1)S(1)}, bf16[768,640]{1,0:T(8,128)(2,1)S(1)}, u32[]{:S(2)}, u32[]{:S(2)}) collective-permute-start(bf16[768,640]{1,0:T(8,128)(2,1)S(1)} %collective-permute-done.near_ref), channel_id=1, source_target_pairs={{0,32},{32,0},{64,96},{96,64},{128,160},{160,128},{192,224},{224,1... | collective-permute-start | bytes 2949128 | tf_op jit(solution)/shard_map/ppermute | solution.py:274
  55.3 1.6 %copy-start.13 = (bf16[768,640]{1,0:T(8,128)(2,1)}, bf16[768,640]{1,0:T(8,128)(2,1)S(1)}, u32[]{:S(2)}) copy-start(bf16[768,640]{1,0:T(8,128)(2,1)S(1)} %collective-permute-done.1.side_ref) | copy-start | bytes 2949124
  55.3 1.0 copy-start.14
  66.1 22.7 %collective-permute-start.3 = (bf16[768,256]{1,0:T(8,128)(2,1)}, bf16[768,256]{1,0:T(8,128)(2,1)S(1)}, u32[]{:S(2)}, u32[]{:S(2)}) collective-permute-start(bf16[768,256]{1,0:T(8,128)(2,1)} %get-tuple-element.44), channel_id=1, source_target_pairs={{0,32},{32,0},{64,96},{96,64},{128,160},{160,128},{192,224},{224,1... | collective-permute-start | bytes 1179656 | tf_op jit(solution)/shard_map/ppermute | solution.py:322
  68.0 20.8 %collective-permute-start.4 = (bf16[768,256]{1,0:T(8,128)(2,1)}, bf16[768,256]{1,0:T(8,128)(2,1)S(1)}, u32[]{:S(2)}, u32[]{:S(2)}) collective-permute-start(bf16[768,256]{1,0:T(8,128)(2,1)} %get-tuple-element.45), channel_id=1, source_target_pairs={{32,0},{64,32},{96,64},{128,96},{160,128},{192,160},{224,192},{256... | collective-permute-start | bytes 1179656 | tf_op jit(solution)/shard_map/ppermute | solution.py:321
  70.5 18.3 %copy-start.7 = (bf16[768,256]{1,0:T(8,128)(2,1)S(1)}, bf16[768,256]{1,0:T(8,128)(2,1)}, u32[]{:S(2)}) copy-start(bf16[768,256]{1,0:T(8,128)(2,1)} %get-tuple-element.43) | copy-start | bytes 1179652
  83.3 13.3 %copy-start.5 = (bf16[768,384]{1,0:T(8,128)(2,1)S(1)}, bf16[768,384]{1,0:T(8,128)(2,1)}, u32[]{:S(2)}) copy-start(bf16[768,384]{1,0:T(8,128)(2,1)} %get-tuple-element.47) | copy-start | bytes 1769476
  83.3 13.3 %collective-permute-start.5 = (bf16[768,384]{1,0:T(8,128)(2,1)}, bf16[768,384]{1,0:T(8,128)(2,1)S(1)}, u32[]{:S(2)}, u32[]{:S(2)}) collective-permute-start(bf16[768,384]{1,0:T(8,128)(2,1)} %get-tuple-element.48), channel_id=1, source_target_pairs={{0,32},{32,0},{64,96},{96,64},{128,160},{160,128},{192,224},{224,1... | collective-permute-start | bytes 1769480 | tf_op jit(solution)/shard_map/ppermute | solution.py:322
  85.3 11.3 %collective-permute-start.6 = (bf16[768,384]{1,0:T(8,128)(2,1)}, bf16[768,384]{1,0:T(8,128)(2,1)S(1)}, u32[]{:S(2)}, u32[]{:S(2)}) collective-permute-start(bf16[768,384]{1,0:T(8,128)(2,1)} %get-tuple-element.49), channel_id=1, source_target_pairs={{32,0},{64,32},{96,64},{128,96},{160,128},{192,160},{224,192},{256... | collective-permute-start | bytes 1769480 | tf_op jit(solution)/shard_map/ppermute | solution.py:321
  88.8 8.1 %copy-start.2 = (bf16[768,256]{1,0:T(8,128)(2,1)}, bf16[768,256]{1,0:T(8,128)(2,1)S(1)}, u32[]{:S(2)}) copy-start(bf16[768,256]{1,0:T(8,128)(2,1)S(1)} %collective-permute-done.4.side_back) | copy-start | bytes 1179652
  89.0 12.0 %all-to-all-start.2 = ((f32[16,1,1664]{2,1,0:T(1,128)}), f32[16,1,1664]{2,1,0:T(1,128)S(1)}, u32[]{:S(2)}, u32[]{:S(2)}) async-start(f32[16,1,1664]{2,1,0:T(1,128)} %get-tuple-element.46), calls=%async_computation.2 | async-start | bytes 212992 | tf_op jit(solution)/shard_map/all_to_all | solution.py:331
  96.6 0.8 copy-start
  101.0 2.3 %copy-start.6 = (f32[16,1,1664]{2,1,0:T(1,128)}, f32[16,1,1664]{2,1,0:T(1,128)S(1)}, u32[]{:S(2)}) copy-start(f32[16,1,1664]{2,1,0:T(1,128)S(1)} %all-to-all-done.2.rows_ref) | copy-start | bytes 319492
  101.0 37.2 %collective-permute-start.7 = (bf16[768,384]{1,0:T(8,128)(2,1)S(1)}, bf16[768,384]{1,0:T(8,128)(2,1)S(1)}, u32[]{:S(2)}, u32[]{:S(2)}) collective-permute-start(bf16[768,384]{1,0:T(8,128)(2,1)S(1)} %add_convert_fusion), channel_id=1, source_target_pairs={{64,0},{96,32},{128,64},{160,96},{192,128},{224,160},{256,192},{28... | collective-permute-start | bytes 1769480 | tf_op jit(solution)/shard_map/ppermute | solution.py:333
  105.0 29.4 %all-to-all-start.3 = ((f32[32,1,2048]{2,1,0:T(1,128)}), f32[32,1,2048]{2,1,0:T(1,128)S(1)}, u32[]{:S(2)}, u32[]{:S(2)}) async-start(f32[32,1,2048]{2,1,0:T(1,128)} %shard_map.123), calls=%async_computation.3 | async-start | bytes 524288 | tf_op jit(solution)/shard_map/all_to_all | solution.py:341
  114.5 19.9 %collective-permute-start.8 = (bf16[768,256]{1,0:T(8,128)(2,1)S(1)}, bf16[768,256]{1,0:T(8,128)(2,1)S(1)}, u32[]{:S(2)}, u32[]{:S(2)}) collective-permute-start(bf16[768,256]{1,0:T(8,128)(2,1)S(1)} %add_convert_fusion.1), channel_id=1, source_target_pairs={{64,0},{96,32},{128,64},{160,96},{192,128},{224,160},{256,192},{28... | collective-permute-start | bytes 1179656 | tf_op jit(solution)/shard_map/ppermute | solution.py:327
  134.4 0.8 copy-start.8
  134.4 0.8 copy-start.1
  138.2 0.8 copy-start.4

commit v2 on v1

v2 whole, which is shorter than its diff:
```python
import functools
import math

import jax
import jax.numpy as jnp
from jax import lax
from jax.experimental import pallas as pl
from jax.experimental.pallas import tpu as pltpu
from jax.sharding import PartitionSpec as P

HD = 128
EPSILON = 1e-06
MASKED = -1e30
STRIP = 48
F32, LOW = jnp.float32, jnp.bfloat16
VMEM_LIMIT = 60 * 1024 * 1024


def along_lanes(row, width):
    return jnp.transpose(jnp.broadcast_to(row, (width, row.shape[1])))


def row_sums(block):
    return jnp.sum(jnp.transpose(block), axis=0, keepdims=True)


def folded(block, op):
    return functools.reduce(op, [block[at : at + 8] for at in range(0, block.shape[0], 8)])


def power_kernel(q_ref, k_ref, power_out):
    slots, width = q_ref.shape[1:]
    for place, ref in enumerate((q_ref, k_ref)):
        total = jnp.zeros((slots, HD), F32)
        for at in range(0, width, HD):
            part = ref[0, :, at : at + HD].astype(F32)
            total += part * part
        row = row_sums(total)
        for device in range(power_out.shape[0]):
            power_out[device, :, place * slots : (place + 1) * slots] = row


def roots_kernel(full_width, tag_ref, power_ref, note_out, q_out):
    slots = q_out.shape[1]
    power = power_ref[0]
    for device in range(1, power_ref.shape[0]):
        power += power_ref[device]
    inverse = 1.0 / jnp.sqrt(power / full_width + EPSILON)
    q_out[...] = inverse[:, :slots]
    lane = lax.broadcasted_iota(jnp.int32, (1, HD), 1)
    valid = tag_ref[1].astype(F32)
    segment = tag_ref[2].astype(F32)
    tags = jnp.where(lane == 0, valid, jnp.where(lane == 1, segment, 0.0))
    for device in range(note_out.shape[0]):
        note_out[device, :, :slots] = inverse[:, slots:]
        note_out[device, :, slots:] = tags


def head_kernel(
    first, last, total_heads, skip, tag_ref, notes, q_inverse, gain_q_ref, gain_k_ref, q_ref, g_ref,
    own_ref, near_ref, side_ref, swap_ref, *rest,
):
    state_in = rest[0] if first else None
    q_out, own_out, near_out, side_out, swap_out, state_out, *rows_out = rest[skip:-6]
    score_ref, grad_ref, weight_low, grad_low, inverse_ref, inner_ref = rest[-6:]
    step = pl.program_id(0)
    slots = q_ref.shape[1]
    width = total_heads * HD
    scale = 1.0 / math.sqrt(HD)
    mine = tag_ref[0]
    even = lax.rem(mine, 2) == 0
    distances = (0, 2, jnp.where(even, 3, 1), jnp.where(even, 1, 3))
    gain_q = gain_q_ref[...]
    gain_k = gain_k_ref[...]
    segment = tag_ref[2].astype(F32)
    others = [jnp.maximum(mine - distance, 0) for distance in distances]

    @pl.when(step == 0)
    def _():
        for slot in range(4):
            inverse_ref[slot] = along_lanes(notes[others[slot], :, :slots], HD)
        inverse_ref[4] = along_lanes(q_inverse[...], HD)
        inner_ref[...] = jnp.zeros_like(inner_ref)
        if first:
            state_out[...] = state_in[...]
        else:
            state_out[...] = jnp.zeros_like(state_out)

    q_unit = q_ref[0].astype(F32) * inverse_ref[4]
    q_norm = (q_unit * gain_q).astype(LOW)
    live = lax.broadcasted_iota(jnp.int32, (slots, HD), 0) < tag_ref[1]
    g_live = jnp.where(live, g_ref[0].astype(F32), 0.0).astype(LOW)
    q_side = jnp.transpose(q_norm)
    g_side = jnp.transpose(g_live)
    lanes = lax.broadcasted_iota(jnp.int32, (STRIP, slots), 0).astype(F32)
    refs = (own_ref, near_ref, side_ref, swap_ref)
    k_norms, limits = [], []
    for slot, ref in enumerate(refs):
        tags = notes[others[slot], :, slots:]
        same = (tags[:, 1:2] == segment) & (mine >= distances[slot])
        limits.append(jnp.where(same, tags[:, 0:1], 0.0))
        k_norm = (ref[:slots, :].astype(F32) * inverse_ref[slot] * gain_k).astype(LOW)
        k_norms.append(k_norm)
        rows = slice(slot * slots, (slot + 1) * slots)
        score_ref[rows, :] = jnp.dot(k_norm, q_side, preferred_element_type=F32)
        grad_ref[rows, :] = jnp.dot(ref[slots:, :], g_side, preferred_element_type=F32)
    strips = [(slot, at) for slot in range(4) for at in range(0, slots, STRIP)]
    top = jnp.full((8, slots), MASKED, F32)
    for slot, at in strips:
        base = slot * slots + at
        included = lanes < limits[slot] - at
        score = jnp.where(included, score_ref[base : base + STRIP, :], MASKED)
        top = jnp.maximum(top, folded(score, jnp.maximum))
    top = jnp.max(top, axis=0, keepdims=True)
    total = jnp.zeros((8, slots), F32)
    delta = jnp.zeros((8, slots), F32)
    for slot, at in strips:
        base = slot * slots + at
        included = lanes < limits[slot] - at
        score = jnp.where(included, score_ref[base : base + STRIP, :], MASKED)
        exponent = jnp.exp((score - top) * scale)
        score_ref[base : base + STRIP, :] = exponent
        total += folded(exponent, jnp.add)
        delta += folded(exponent * grad_ref[base : base + STRIP, :], jnp.add)
    inverse_sum = 1.0 / jnp.sum(total, axis=0, keepdims=True)
    delta = jnp.sum(delta, axis=0, keepdims=True) * inverse_sum
    q_turned = jnp.zeros((HD, slots), F32)
    k_gain = jnp.zeros((1, HD), F32)
    for slot, out in enumerate((own_out, near_out, side_out, swap_out)):
        for at in range(0, slots, STRIP):
            rows = slice(slot * slots + at, slot * slots + at + STRIP)
            weight = score_ref[rows, :] * inverse_sum
            weight_low[rows, :] = weight.astype(LOW)
            grad_low[rows, :] = (weight * (grad_ref[rows, :] - delta)).astype(LOW)
        rows = slice(slot * slots, (slot + 1) * slots)
        q_turned += jnp.dot(
            jnp.transpose(k_norms[slot]), grad_low[rows, :], preferred_element_type=F32
        )
        k_part = jnp.dot(grad_low[rows, :], q_norm, preferred_element_type=F32) * scale
        v_part = jnp.dot(weight_low[rows, :], g_live, preferred_element_type=F32)
        out[:slots, :] = k_part.astype(out.dtype)
        out[slots:, :] = v_part.astype(out.dtype)
        product = k_part * (refs[slot][:slots, :].astype(F32) * inverse_ref[slot])
        k_gain += jnp.sum(product, axis=0, keepdims=True)
        inner_ref[slot] += product * gain_k
    q_part = jnp.transpose(q_turned) * scale
    q_out[...] = q_part
    product = q_part * q_unit
    inner_ref[4] += product * gain_q
    at = (first + step) * HD
    state_out[5:6, pl.ds(pl.multiple_of(at, HD), HD)] = jnp.sum(product, axis=0, keepdims=True)
    state_out[5:6, pl.ds(pl.multiple_of(width + at, HD), HD)] = k_gain

    @pl.when(step == last - first - 1)
    def _():
        for slot in range(5):
            state_out[slot : slot + 1, :slots] += row_sums(inner_ref[slot])
        if last == total_heads:
            (rows_ref,) = rows_out
            for device in range(rows_ref.shape[0]):
                rows_ref[device, :, :slots] = jnp.zeros((1, slots), F32)
                rows_ref[device, :, slots:] = state_out[5:6, :]
            for slot, distance in enumerate(distances):
                @pl.when(mine >= distance)
                def _():
                    rows_ref[mine - distance, :, :slots] = state_out[slot : slot + 1, :slots]


def head_blocks(first, rows):
    return pl.BlockSpec((rows, HD), lambda head: (0, first + head))


def raw_blocks(first, slots):
    return pl.BlockSpec((1, slots, HD), lambda head: (0, 0, first + head))


def all_of(shape):
    return pl.BlockSpec(shape, lambda *_: (0,) * len(shape))


def attend(
    first, last, chunk, heads, groups, tags, notes, q_inverse, gain_q, gain_k, q, g, halo, state, outs
):
    slots = q.shape[1]
    width = (chunk[1] - chunk[0]) * HD
    place = first - chunk[0]
    state_shape = (8, 2 * heads * HD)
    row_shape = (groups, 1, slots + 2 * heads * HD)
    final = last == heads
    known = 11 + len(state)
    return pl.pallas_call(
        functools.partial(head_kernel, first, last, heads, len(state) + len(outs)),
        grid=(last - first,),
        in_specs=[
            pl.BlockSpec(memory_space=pltpu.SMEM),
            all_of(notes.shape),
            all_of((1, slots)),
            head_blocks(first, 1),
            head_blocks(first, 1),
            raw_blocks(first, slots),
            raw_blocks(first, slots),
            *[head_blocks(first, 2 * slots)] * 4,
            *[all_of(state_shape)] * len(state),
            *[pl.BlockSpec(memory_space=pl.ANY)] * len(outs),
        ],
        out_specs=[
            head_blocks(place, slots),
            *[head_blocks(place, 2 * slots)] * 4,
            all_of(state_shape),
            *[all_of(row_shape)] * final,
        ],
        out_shape=[
            struct((slots, width)),
            struct((2 * slots, width)),
            *[struct((2 * slots, width), LOW)] * 3,
            struct(state_shape),
            *[struct(row_shape)] * final,
        ],
        scratch_shapes=[
            pltpu.VMEM((4 * slots, slots), F32),
            pltpu.VMEM((4 * slots, slots), F32),
            pltpu.VMEM((4 * slots, slots), LOW),
            pltpu.VMEM((4 * slots, slots), LOW),
            pltpu.VMEM((5, slots, HD), F32),
            pltpu.VMEM((5, slots, HD), F32),
        ],
        input_output_aliases={known + i: i for i in range(len(outs))},
        compiler_params=kernel_params(),
        cost_estimate=pl.CostEstimate(
            flops=(last - first) * 40 * slots * slots * HD,
            bytes_accessed=(last - first) * 44 * slots * HD,
            transcendentals=(last - first) * 4 * slots * slots,
        ),
    )(tags, notes, q_inverse, gain_q, gain_k, q, g, *halo, *state, *outs)


def collect_kernel(state_ref, rows_ref, inner_out, gain_out):
    slots = inner_out.shape[2] // 2
    total = rows_ref[0]
    for device in range(1, rows_ref.shape[0]):
        total += rows_ref[device]
    for device in range(inner_out.shape[0]):
        inner_out[device, :, :slots] = state_ref[4:5, :slots]
        inner_out[device, :, slots:] = total[:, :slots]
    for device in range(gain_out.shape[0]):
        gain_out[device] = total[:, slots:]


def total_of(sums):
    total = sums[0]
    for other in range(1, sums.shape[0]):
        total += sums[other]
    return total


def query_kernel(
    full_width, q_inverse, gain_ref, inners, q_ref, q_part, query_out, turned
):
    rows, width = q_ref.shape[1:]
    slots = q_inverse.shape[1]
    step = pl.program_id(0)

    @pl.when(step == 0)
    def _():
        inner = total_of(inners)[:, :slots] / full_width
        turned[0] = along_lanes(q_inverse[...], HD)
        turned[1] = along_lanes(inner, HD) * turned[0]

    here = pl.ds(pl.multiple_of(step * rows, 16), rows)
    inverse, inner = turned[0, here, :], turned[1, here, :]
    for at in range(0, width, HD):
        lanes = slice(at, at + HD)
        scaled = q_part[:, lanes] * gain_ref[:, lanes]
        query_out[0, :, lanes] = ((scaled - q_ref[0, :, lanes].astype(F32) * inner) * inverse).astype(LOW)


def key_kernel(
    full_width, tag_ref, notes, gain_ref, inners, k_ref, k_own, v_own, k_side, v_side, k_near,
    v_near, key_out, value_out, turned,
):
    rows, width = k_ref.shape[1:]
    slots = turned.shape[1]
    mine = tag_ref[0]
    step = pl.program_id(0)

    @pl.when(step == 0)
    def _():
        inner = total_of(inners)[:, slots:] / full_width
        turned[0] = along_lanes(notes[mine, :, :slots], HD)
        turned[1] = along_lanes(inner, HD) * turned[0]

    here = pl.ds(pl.multiple_of(step * rows, 16), rows)
    inverse, inner = turned[0, here, :], turned[1, here, :]
    keep = jnp.where(lax.rem(mine, 2) == 0, 1.0, 0.0)
    for at in range(0, width, HD):
        lanes = slice(at, at + HD)
        total = k_own[:, lanes] + k_near[:, lanes].astype(F32)
        total += k_side[:, lanes].astype(F32) * keep
        scaled = total * gain_ref[:, lanes]
        key_out[0, :, lanes] = ((scaled - k_ref[0, :, lanes].astype(F32) * inner) * inverse).astype(LOW)
        total = v_own[:, lanes] + v_near[:, lanes].astype(F32)
        value_out[0, :, lanes] = (total + v_side[:, lanes].astype(F32) * keep).astype(LOW)


def struct(shape, dtype=F32):
    return jax.ShapeDtypeStruct(shape, dtype)


def kernel_params(limit=VMEM_LIMIT):
    return pltpu.CompilerParams(vmem_limit_bytes=limit)


def on_device(q_proj, k_proj, values, grad_out, gain_q, gain_k, valid_count, segment):
    _, slots, local_width = q_proj.shape
    heads = local_width // HD
    mp_size, dp_size = lax.axis_size("mp"), lax.axis_size("dp")
    full_width = local_width * mp_size
    groups = lax.axis_size("tm")
    mine = lax.axis_index("tm")
    even = mine % 2 == 0
    tags = jnp.stack([mine, valid_count[0, 0], segment[0, 0]]).astype(jnp.int32)
    gain_q = gain_q.reshape(1, local_width)
    gain_k = gain_k.reshape(1, local_width)
    smem = pl.BlockSpec(memory_space=pltpu.SMEM)

    two_on = [(i, i + 2) for i in range(groups - 2)]
    one_on = [(i, i + 1) for i in range(groups - 1)]
    pair = [(i, i ^ 1) for i in range(groups)]
    back = lambda moves: [(there, here) for here, there in moves]

    anywhere = pl.BlockSpec(memory_space=pl.ANY)
    own = jnp.concatenate([k_proj[0], values[0]], axis=0)
    near = lax.ppermute(own, "tm", two_on)
    power = pl.pallas_call(
        power_kernel,
        out_shape=struct((mp_size, 1, 2 * slots)),
        compiler_params=kernel_params(),
        cost_estimate=pl.CostEstimate(flops=10**6, bytes_accessed=10**6, transcendentals=0),
    )(q_proj, k_proj)
    powers = lax.all_to_all(power, "mp", 0, 0, tiled=True)
    note, q_inverse = pl.pallas_call(
        functools.partial(roots_kernel, full_width),
        in_specs=[smem, pl.BlockSpec()],
        out_shape=[struct((groups, 1, slots + HD)), struct((1, slots))],
        compiler_params=kernel_params(),
    )(tags, powers)
    near, note = lax.optimization_barrier((near, note))
    passed, note = lax.optimization_barrier((jnp.where(even, own, near), note))
    side = lax.ppermute(passed, "tm", one_on)
    swap = lax.ppermute(near, "tm", pair)
    notes = lax.all_to_all(note, "tm", 0, 0, tiled=True)

    q_part, own_part, near_part, side_part, swap_part, state, rows = attend(
        0, heads, (0, heads), heads, groups, tags, notes, q_inverse, gain_q, gain_k, q_proj,
        grad_out, (own, near, side, swap), [], [],
    )
    side_back = lax.ppermute(side_part, "tm", back(one_on))
    swap_back = lax.ppermute(swap_part, "tm", pair)
    rows = lax.all_to_all(rows, "tm", 0, 0, tiled=True)
    inners, gains = pl.pallas_call(
        collect_kernel,
        out_shape=[struct((mp_size, 1, 2 * slots)), struct((dp_size, 1, 2 * local_width))],
        compiler_params=kernel_params(),
    )(state, rows)
    near_sum = near_part.astype(F32) + swap_back.astype(F32)
    near_sum = (near_sum + jnp.where(even, 0.0, side_back.astype(F32))).astype(LOW)
    inners, near_sum = lax.optimization_barrier((inners, near_sum))
    near_back = lax.ppermute(near_sum, "tm", back(two_on))
    inners = lax.all_to_all(inners, "mp", 0, 0, tiled=True)
    gains, inners = lax.optimization_barrier((gains, inners))
    gains = lax.all_to_all(gains, "dp", 0, 0, tiled=True)

    steps = 4
    block = slots // steps
    raw = pl.BlockSpec((1, block, local_width), lambda step: (0, step, 0))
    upper = pl.BlockSpec((block, local_width), lambda step: (step, 0))
    lower = pl.BlockSpec((block, local_width), lambda step: (step + steps, 0))
    query_grad = pl.pallas_call(
        functools.partial(query_kernel, full_width),
        grid=(steps,),
        in_specs=[
            all_of((1, slots)),
            all_of((1, local_width)),
            all_of(inners.shape),
            raw,
            upper,
        ],
        out_specs=raw,
        out_shape=struct(q_proj.shape, LOW),
        scratch_shapes=[pltpu.VMEM((2, slots, HD), F32)],
        compiler_params=kernel_params(16 * 1024 * 1024),
        cost_estimate=pl.CostEstimate(flops=10**6, bytes_accessed=3 * 10**6, transcendentals=0),
    )(q_inverse, gain_q, inners, q_proj, q_part)
    key_grad, value_grad = pl.pallas_call(
        functools.partial(key_kernel, full_width),
        grid=(steps,),
        in_specs=[
            smem,
            all_of(notes.shape),
            all_of((1, local_width)),
            all_of(inners.shape),
            raw,
            *[upper, lower] * 3,
        ],
        out_specs=[raw] * 2,
        out_shape=[struct(q_proj.shape, LOW)] * 2,
        scratch_shapes=[pltpu.VMEM((2, slots, HD), F32)],
        compiler_params=kernel_params(16 * 1024 * 1024),
        cost_estimate=pl.CostEstimate(flops=10**6, bytes_accessed=5 * 10**6, transcendentals=0),
    )(
        tags, notes, gain_k, inners, k_proj,
        own_part, own_part, side_back, side_back, near_back, near_back,
    )
    gain_sum = jnp.sum(gains[:, 0], axis=0)
    return query_grad, key_grad, value_grad, gain_sum[:local_width], gain_sum[local_width:]


def solution(mesh):
    wide = P("dp", "tm", "mp")
    in_specs = (wide, wide, wide, wide, P("mp"), P("mp"), P("dp", "tm"), P("dp", "tm"))
    out_specs = (wide, wide, wide, P("mp"), P("mp"))
    return jax.shard_map(
        on_device, mesh=mesh, in_specs=in_specs, out_specs=out_specs, check_vma=False
    )
```

time: 146 us -> 135 us (0.925)
  the two profiles are of different devices: /device:TPU:6 before, /device:TPU:8 now
where the time goes in v2:
time: 135 us; the launch traced here: 134 us
  starting transfers between devices  38 us (28%)
  blocking collectives  33.4 us (25%)
  Pallas kernels  29.7 us (22%)
  waiting for transfers between devices  18.8 us (14%)
  other arithmetic  5.89 us (4%)
  local copies, waits for them, and re-layouts  5.57 us (4%)
  between operations  2.15 us (2%)
    pallas_call x1, Pallas kernels, attend(): pl.pallas_call(functools.partial(head_kernel, first, last, heads, len(sta...  19.3 us
    all_to_all x1, blocking collectives, on_device(): inners = lax.all_to_all(inners, 'mp', 0, 0, tiled=True)  17.9 us
    all_to_all x1, blocking collectives, on_device(): rows = lax.all_to_all(rows, 'tm', 0, 0, tiled=True)  15.4 us
    all_to_all x1, starting transfers between devices, on_device(): powers = lax.all_to_all(power, 'mp', 0, 0, tiled=True)  10.3 us
    all_to_all x1, waiting for transfers between devices, on_device(): notes = lax.all_to_all(note, 'tm', 0, 0, tiled=True)  7.04 us
    all_to_all x1, starting transfers between devices, on_device(): notes = lax.all_to_all(note, 'tm', 0, 0, tiled=True)  6.09 us
    all_to_all x1, starting transfers between devices, on_device(): gains = lax.all_to_all(gains, 'dp', 0, 0, tiled=True)  6.05 us
    all_to_all x1, waiting for transfers between devices, on_device(): powers = lax.all_to_all(power, 'mp', 0, 0, tiled=True)  5.93 us
  transfers between devices with their start and end apart: 9, of which 4 were waited for; matrix products, arithmetic and copies ran while one was open for 2% of the time, Pallas kernels for 5%

profile of v2, /device:TPU:8, one launch (start us, length us, event | category | flops | bytes accessed | tf_op | source)
XLA Modules:
  0.0 133.6 jit_solution(13723165230509892782)
XLA Ops:
  0.6 0.0 copy-start
  0.7 1.3 %pad_maximum_fusion.own_ref = bf16[768,640]{1,0:T(8,128)(2,1)S(1)} fusion(bf16[384,640]{1,0:T(8,128)(2,1)} %bitcast.9, bf16[384,640]{1,0:T(8,128)(2,1)} %bitcast.7), kind=kLoop, calls=%fused_computation.1 | loop fusion | flops 1966080 | bytes 1966080 | tf_op jit(solution)/shard_map/concatenate | solution.py:332
  2.0 0.0 copy-start.11
  2.0 0.0 copy-start.15
  2.0 0.0 copy-start.16
  2.0 3.5 %collective-permute-start = (bf16[768,640]{1,0:T(8,128)(2,1)S(1)}, bf16[768,640]{1,0:T(8,128)(2,1)S(1)}, u32[]{:S(2)}, u32[]{:S(2)}) collective-permute-start(bf16[768,640]{1,0:T(8,128)(2,1)S(1)} %pad_maximum_fusion.own_ref), channel_id=1, source_target_pairs={{0,64},{32,96},{64,128},{96,160},{128,192},{160,224},{192,256},{22... | collective-permute-start | bytes 2949128 | tf_op jit(solution)/shard_map/ppermute | solution.py:333
  5.6 2.1 %shard_map.119 = f32[8,1,768]{2,1,0:T(1,128)} custom-call(bf16[1,384,640]{2,1,0:T(8,128)(2,1)} %q_ref.5, bf16[1,384,640]{2,1,0:T(8,128)(2,1)} %k_ref.3), custom_call_target="tpu_custom_call" | custom-call | flops 1000000 | bytes 1000000 | tf_op jit(solution)/shard_map/pallas_call | solution.py:334
  7.6 10.3 %all-to-all-start = ((f32[8,1,768]{2,1,0:T(1,128)}), f32[8,1,768]{2,1,0:T(1,128)S(1)}, u32[]{:S(2)}, u32[]{:S(2)}) async-start(f32[8,1,768]{2,1,0:T(1,128)} %shard_map.119), calls=%async_computation | async-start | bytes 49152 | tf_op jit(solution)/shard_map/all_to_all | solution.py:340
  19.2 0.6 pad_add_fusion.tag_ref
  19.8 5.9 %all-to-all-done.power_ref = f32[8,1,768]{2,1,0:T(1,128)S(1)} async-done(((f32[8,1,768]{2,1,0:T(1,128)}), f32[8,1,768]{2,1,0:T(1,128)S(1)}, u32[]{:S(2)}, u32[]{:S(2)}) %all-to-all-start) | async-done | bytes 24608 | tf_op jit(solution)/shard_map/all_to_all | solution.py:340
  25.8 0.6 copy-done.13
  26.4 1.4 %shard_map.120 = (f32[16,1,512]{2,1,0:T(1,128)}, f32[1,384]{1,0:T(1,128)}) custom-call(s32[3]{0:T(128)} %pad_add_fusion.tag_ref, f32[8,1,768]{2,1,0:T(1,128)} %copy-done.13), custom_call_target="tpu_custom_call" | custom-call | tf_op jit(solution)/shard_map/pallas_call | solution.py:341
  27.8 1.9 %collective-permute-done.near_ref = bf16[768,640]{1,0:T(8,128)(2,1)S(1)} collective-permute-done((bf16[768,640]{1,0:T(8,128)(2,1)S(1)}, bf16[768,640]{1,0:T(8,128)(2,1)S(1)}, u32[]{:S(2)}, u32[]{:S(2)}) %collective-permute-start) | collective-permute-done | bytes 983072 | tf_op jit(solution)/shard_map/ppermute | solution.py:333
  29.7 1.4 %broadcast_select_fusion = bf16[768,640]{1,0:T(8,128)(2,1)} fusion(bf16[768,640]{1,0:T(8,128)(2,1)S(1)} %collective-permute-done.near_ref, pred[]{:T(512)S(6)} %eq.5, bf16[384,640]{1,0:T(8,128)(2,1)S(1)} %bitcast.10, bf16[384,640]{1,0:T(8,128)(2,1)S(1)} %bitcast.8), kind=kLoop, calls=%fused_computation.2 | loop fusion | flops 2457600 | bytes 2949121 | tf_op jit(solution)/shard_map/jit(_where)/select_n | solution.py:348
  31.0 1.9 %collective-permute-start.1 = (bf16[768,640]{1,0:T(8,128)(2,1)}, bf16[768,640]{1,0:T(8,128)(2,1)}, u32[]{:S(2)}, u32[]{:S(2)}) collective-permute-start(bf16[768,640]{1,0:T(8,128)(2,1)} %broadcast_select_fusion), channel_id=1, source_target_pairs={{0,32},{32,64},{64,96},{96,128},{128,160},{160,192},{192,224},{224... | collective-permute-start | bytes 2949128 | tf_op jit(solution)/shard_map/ppermute | solution.py:349
  32.9 1.9 %collective-permute-start.2 = (bf16[768,640]{1,0:T(8,128)(2,1)S(1)}, bf16[768,640]{1,0:T(8,128)(2,1)S(1)}, u32[]{:S(2)}, u32[]{:S(2)}) collective-permute-start(bf16[768,640]{1,0:T(8,128)(2,1)S(1)} %collective-permute-done.near_ref), channel_id=1, source_target_pairs={{0,32},{32,0},{64,96},{96,64},{128,160},{160,128},{192,224},{224,1... | collective-permute-start | bytes 2949128 | tf_op jit(solution)/shard_map/ppermute | solution.py:350
  34.9 6.1 %all-to-all-start.1 = ((f32[16,1,512]{2,1,0:T(1,128)}), f32[16,1,512]{2,1,0:T(1,128)S(1)}, u32[]{:S(2)}, u32[]{:S(2)}) async-start(f32[16,1,512]{2,1,0:T(1,128)} %get-tuple-element.30), calls=%async_computation.1 | async-start | bytes 65536 | tf_op jit(solution)/shard_map/all_to_all | solution.py:351
  41.0 0.6 reshape.16.gain_q_ref.gain_ref
  41.6 0.6 reshape.17.gain_k_ref.gain_ref
  42.1 7.0 %all-to-all-done.1.notes = f32[16,1,512]{2,1,0:T(1,128)S(1)} async-done(((f32[16,1,512]{2,1,0:T(1,128)}), f32[16,1,512]{2,1,0:T(1,128)S(1)}, u32[]{:S(2)}, u32[]{:S(2)}) %all-to-all-start.1) | async-done | bytes 32800 | tf_op jit(solution)/shard_map/all_to_all | solution.py:351
  49.2 0.0 collective-permute-done.1.side_ref
  49.2 0.0 collective-permute-done.2.swap_ref
  49.2 0.6 copy-done.4
  49.8 0.3 copy-done.17
  50.1 19.3 %shard_map.121 = (f32[384,640]{1,0:T(8,128)}, f32[768,640]{1,0:T(8,128)}, bf16[768,640]{1,0:T(8,128)(2,1)}, bf16[768,640]{1,0:T(8,128)(2,1)}, bf16[768,640]{1,0:...) custom-call(s32[3]{0:T(128)} %pad_add_fusion.tag_ref, f32[16,1,512]{2,1,0:T(1,128)} %copy-done.4, ...), custom_call_target="tpu_custom_call" | custom-call | flops 3774873600 | bytes 10813440 | tf_op jit(solution)/shard_map/pallas_call | solution.py:191
  69.4 2.0 %collective-permute-start.3 = (bf16[768,640]{1,0:T(8,128)(2,1)}, bf16[768,640]{1,0:T(8,128)(2,1)S(1)}, u32[]{:S(2)}, u32[]{:S(2)}) collective-permute-start(bf16[768,640]{1,0:T(8,128)(2,1)} %get-tuple-element.37), channel_id=1, source_target_pairs={{0,32},{32,0},{64,96},{96,64},{128,160},{160,128},{192,224},{224,1... | collective-permute-start | bytes 2949128 | tf_op jit(solution)/shard_map/ppermute | solution.py:358
  71.4 1.9 %collective-permute-start.4 = (bf16[768,640]{1,0:T(8,128)(2,1)}, bf16[768,640]{1,0:T(8,128)(2,1)S(1)}, u32[]{:S(2)}, u32[]{:S(2)}) collective-permute-start(bf16[768,640]{1,0:T(8,128)(2,1)} %get-tuple-element.38), channel_id=1, source_target_pairs={{32,0},{64,32},{96,64},{128,96},{160,128},{192,160},{224,192},{256... | collective-permute-start | bytes 2949128 | tf_op jit(solution)/shard_map/ppermute | solution.py:357
  73.3 15.4 %all_to_all.25.rows_ref = f32[16,1,1664]{2,1,0:T(1,128)} all-to-all(f32[16,1,1664]{2,1,0:T(1,128)} %get-tuple-element.33), channel_id=1, replica_groups=mesh['tm'=16,'mp'=8,'dp'=4] {'tm'}, dimensions={0} | all-to-all | bytes 212992 | tf_op jit(solution)/shard_map/all_to_all | solution.py:359
  88.7 1.5 %shard_map.122 = (f32[8,1,768]{2,1,0:T(1,128)}, f32[4,1,1280]{2,1,0:T(1,128)}) custom-call(f32[8,1280]{1,0:T(8,128)} %get-tuple-element.32.state_ref, f32[16,1,1664]{2,1,0:T(1,128)} %all_to_all.25.rows_ref), custom_call_target="tpu_custom_call" | custom-call | tf_op jit(solution)/shard_map/pallas_call | solution.py:360
  90.3 0.0 collective-permute-done.3
  90.3 0.0 collective-permute-done.4.k_side.v_side
  90.3 0.0 copy-start.14
  90.3 0.0 copy-start.6
  90.3 0.0 copy-start.9
  90.3 0.0 copy-start.5
  90.3 0.0 copy-start.7
  90.3 0.0 copy-start.8
  90.3 2.6 %add_convert_fusion = bf16[768,640]{1,0:T(8,128)(2,1)} fusion(bf16[768,640]{1,0:T(8,128)(2,1)S(1)} %collective-permute-done.4.k_side.v_side, bf16[768,640]{1,0:T(8,128)(2,1)S(1)} %collective-permute-done.3, bf16[768,640]{1,0:T(8,128)(2,1)} %get-tuple-element.36, pred[]{:T(512)S(6)} %eq.5), kind=kLoop, calls=%fused_computation | loop fusion | flops 3440640 | bytes 3932161 | tf_op jit(solution)/shard_map/convert_element_type | solution.py:366
  92.9 4.3 %collective-permute-start.5 = (bf16[768,640]{1,0:T(8,128)(2,1)}, bf16[768,640]{1,0:T(8,128)(2,1)}, u32[]{:S(2)}, u32[]{:S(2)}) collective-permute-start(bf16[768,640]{1,0:T(8,128)(2,1)} %add_convert_fusion), channel_id=1, source_target_pairs={{64,0},{96,32},{128,64},{160,96},{192,128},{224,160},{256,192},{28... | collective-permute-start | bytes 2949128 | tf_op jit(solution)/shard_map/ppermute | solution.py:368
  97.3 17.9 %all_to_all.26.inners = f32[8,1,768]{2,1,0:T(1,128)S(1)} all-to-all(f32[8,1,768]{2,1,0:T(1,128)S(1)} %copy-done.14), channel_id=1, replica_groups=mesh['tm'=16,'mp'=8,'dp'=4] {'mp'}, dimensions={0} | all-to-all | bytes 49152 | tf_op jit(solution)/shard_map/all_to_all | solution.py:369
  115.2 6.0 %all-to-all-start.4 = ((f32[4,1,1280]{2,1,0:T(1,128)}), f32[4,1,1280]{2,1,0:T(1,128)S(1)}, u32[]{:S(2)}, u32[]{:S(2)}) async-start(f32[4,1,1280]{2,1,0:T(1,128)} %get-tuple-element.46), calls=%async_computation.4 | async-start | bytes 40960 | tf_op jit(solution)/shard_map/all_to_all | solution.py:371
  121.3 1.0 copy-done.2
  122.3 1.2 copy-done.3
  123.5 1.6 %shard_map.123 = bf16[1,384,640]{2,1,0:T(8,128)(2,1)} custom-call(f32[1,384]{1,0:T(1,128)S(1)} %copy-done.9, f32[1,640]{1,0:T(1,128)S(1)} %copy-done.6, f32[8,1,768]{2,1,0:T(1,128)S(1)} %all_to_all.26.inners, bf16[1,384,640]{2,1,0:T(8,128)(2,1)S(1)} %copy-done.2, f32[384,640]{1,0:T(8,128)S(1)} %copy-done.3), custom_call_target="tpu_custom_call" | custom-call | flops 1000000 | bytes 3000000 | tf_op jit(solution)/shard_map/pallas_call | solution.py:378
  125.1 3.9 %all-to-all-done.4 = f32[4,1,1280]{2,1,0:T(1,128)S(1)} async-done(((f32[4,1,1280]{2,1,0:T(1,128)}), f32[4,1,1280]{2,1,0:T(1,128)S(1)}, u32[]{:S(2)}, u32[]{:S(2)}) %all-to-all-start.4) | async-done | bytes 20512 | tf_op jit(solution)/shard_map/all_to_all | solution.py:371
  129.1 0.6 fusion
  129.7 0.0 collective-permute-done.5.k_near.v_near
  129.7 3.8 %shard_map.124 = (bf16[1,384,640]{2,1,0:T(8,128)(2,1)}, bf16[1,384,640]{2,1,0:T(8,128)(2,1)}) custom-call(s32[3]{0:T(128)S(1)} %copy-done.8, f32[16,1,512]{2,1,0:T(1,128)S(1)} %copy-done.5, f32[1,640]{1,0:T(1,128)S(1)} %copy-done.7, f32[8,1,768]{2,1,0:T(1,128)S(1)} %all_to_all.26.inners, bf16[1,384,640]{2,1,0:T(8,128)(2,1)S(1)} %copy-done, ...), custom_call_target="tpu_custom_call" | custom-call | flops 1000000 | bytes 5000000 | tf_op jit(solution)/shard_map/pallas_call | solution.py:394
  (22 shorter events, 0.1 us)
Async XLA Ops:
  0.6 29.0 %copy-start = (bf16[1,384,640]{2,1,0:T(8,128)(2,1)S(1)}, bf16[1,384,640]{2,1,0:T(8,128)(2,1)}, u32[]{:S(2)}) copy-start(bf16[1,384,640]{2,1,0:T(8,128)(2,1)} %k_ref.3) | copy-start | bytes 1474564
  0.6 29.0 %copy-start.10 = (bf16[1,384,640]{2,1,0:T(8,128)(2,1)S(1)}, bf16[1,384,640]{2,1,0:T(8,128)(2,1)}, u32[]{:S(2)}) copy-start(bf16[1,384,640]{2,1,0:T(8,128)(2,1)} %param.10) | copy-start | bytes 1474564
  2.0 29.0 %copy-start.11 = (bf16[768,640]{1,0:T(8,128)(2,1)}, bf16[768,640]{1,0:T(8,128)(2,1)S(1)}, u32[]{:S(2)}) copy-start(bf16[768,640]{1,0:T(8,128)(2,1)S(1)} %pad_maximum_fusion.own_ref) | copy-start | bytes 2949124
  2.0 39.0 %copy-start.15 = (f32[640]{0:T(1024)S(1)}, f32[640]{0:T(1024)}, u32[]{:S(2)}) copy-start(f32[640]{0:T(1024)} %param.12) | copy-start | bytes 7684
  2.0 39.5 %copy-start.16 = (f32[640]{0:T(1024)S(1)}, f32[640]{0:T(1024)}, u32[]{:S(2)}) copy-start(f32[640]{0:T(1024)} %param.13) | copy-start | bytes 7684
  2.0 27.6 %collective-permute-start = (bf16[768,640]{1,0:T(8,128)(2,1)S(1)}, bf16[768,640]{1,0:T(8,128)(2,1)S(1)}, u32[]{:S(2)}, u32[]{:S(2)}) collective-permute-start(bf16[768,640]{1,0:T(8,128)(2,1)S(1)} %pad_maximum_fusion.own_ref), channel_id=1, source_target_pairs={{0,64},{32,96},{64,128},{96,160},{128,192},{160,224},{192,256},{22... | collective-permute-start | bytes 2949128 | tf_op jit(solution)/shard_map/ppermute | solution.py:333
  7.6 18.1 %all-to-all-start = ((f32[8,1,768]{2,1,0:T(1,128)}), f32[8,1,768]{2,1,0:T(1,128)S(1)}, u32[]{:S(2)}, u32[]{:S(2)}) async-start(f32[8,1,768]{2,1,0:T(1,128)} %shard_map.119), calls=%async_computation | async-start | bytes 49152 | tf_op jit(solution)/shard_map/all_to_all | solution.py:340
  25.8 0.6 copy-start.13
  29.7 19.5 %copy-start.12 = (bf16[768,640]{1,0:T(8,128)(2,1)}, bf16[768,640]{1,0:T(8,128)(2,1)S(1)}, u32[]{:S(2)}) copy-start(bf16[768,640]{1,0:T(8,128)(2,1)S(1)} %collective-permute-done.near_ref) | copy-start | bytes 2949124
  31.0 18.1 %collective-permute-start.1 = (bf16[768,640]{1,0:T(8,128)(2,1)}, bf16[768,640]{1,0:T(8,128)(2,1)}, u32[]{:S(2)}, u32[]{:S(2)}) collective-permute-start(bf16[768,640]{1,0:T(8,128)(2,1)} %broadcast_select_fusion), channel_id=1, source_target_pairs={{0,32},{32,64},{64,96},{96,128},{128,160},{160,192},{192,224},{224... | collective-permute-start | bytes 2949128 | tf_op jit(solution)/shard_map/ppermute | solution.py:349
  32.9 16.2 %collective-permute-start.2 = (bf16[768,640]{1,0:T(8,128)(2,1)S(1)}, bf16[768,640]{1,0:T(8,128)(2,1)S(1)}, u32[]{:S(2)}, u32[]{:S(2)}) collective-permute-start(bf16[768,640]{1,0:T(8,128)(2,1)S(1)} %collective-permute-done.near_ref), channel_id=1, source_target_pairs={{0,32},{32,0},{64,96},{96,64},{128,160},{160,128},{192,224},{224,1... | collective-permute-start | bytes 2949128 | tf_op jit(solution)/shard_map/ppermute | solution.py:350
  34.9 14.3 %all-to-all-start.1 = ((f32[16,1,512]{2,1,0:T(1,128)}), f32[16,1,512]{2,1,0:T(1,128)S(1)}, u32[]{:S(2)}, u32[]{:S(2)}) async-start(f32[16,1,512]{2,1,0:T(1,128)} %get-tuple-element.30), calls=%async_computation.1 | async-start | bytes 65536 | tf_op jit(solution)/shard_map/all_to_all | solution.py:351
  49.2 0.6 copy-start.4
  49.2 0.9 copy-start.17
  69.4 20.9 %collective-permute-start.3 = (bf16[768,640]{1,0:T(8,128)(2,1)}, bf16[768,640]{1,0:T(8,128)(2,1)S(1)}, u32[]{:S(2)}, u32[]{:S(2)}) collective-permute-start(bf16[768,640]{1,0:T(8,128)(2,1)} %get-tuple-element.37), channel_id=1, source_target_pairs={{0,32},{32,0},{64,96},{96,64},{128,160},{160,128},{192,224},{224,1... | collective-permute-start | bytes 2949128 | tf_op jit(solution)/shard_map/ppermute | solution.py:358
  71.4 18.9 %collective-permute-start.4 = (bf16[768,640]{1,0:T(8,128)(2,1)}, bf16[768,640]{1,0:T(8,128)(2,1)S(1)}, u32[]{:S(2)}, u32[]{:S(2)}) collective-permute-start(bf16[768,640]{1,0:T(8,128)(2,1)} %get-tuple-element.38), channel_id=1, source_target_pairs={{32,0},{64,32},{96,64},{128,96},{160,128},{192,160},{224,192},{256... | collective-permute-start | bytes 2949128 | tf_op jit(solution)/shard_map/ppermute | solution.py:357
  90.3 7.0 %copy-start.14 = (f32[8,1,768]{2,1,0:T(1,128)S(1)}, f32[8,1,768]{2,1,0:T(1,128)}, u32[]{:S(2)}) copy-start(f32[8,1,768]{2,1,0:T(1,128)} %get-tuple-element.39) | copy-start | bytes 73732
  90.3 31.0 %copy-start.6 = (f32[1,640]{1,0:T(1,128)S(1)}, f32[1,640]{1,0:T(1,128)}, u32[]{:S(2)}) copy-start(f32[1,640]{1,0:T(1,128)} %reshape.16.gain_q_ref.gain_ref) | copy-start | bytes 7684
  90.3 31.0 %copy-start.9 = (f32[1,384]{1,0:T(1,128)S(1)}, f32[1,384]{1,0:T(1,128)}, u32[]{:S(2)}) copy-start(f32[1,384]{1,0:T(1,128)} %get-tuple-element.26.q_inverse) | copy-start | bytes 4612
  90.3 39.4 %copy-start.5 = (f32[16,1,512]{2,1,0:T(1,128)S(1)}, f32[16,1,512]{2,1,0:T(1,128)}, u32[]{:S(2)}) copy-start(f32[16,1,512]{2,1,0:T(1,128)} %copy-done.4) | copy-start | bytes 98308
  90.3 39.4 %copy-start.7 = (f32[1,640]{1,0:T(1,128)S(1)}, f32[1,640]{1,0:T(1,128)}, u32[]{:S(2)}) copy-start(f32[1,640]{1,0:T(1,128)} %reshape.17.gain_k_ref.gain_ref) | copy-start | bytes 7684
  90.3 39.4 %copy-start.8 = (s32[3]{0:T(128)S(1)}, s32[3]{0:T(128)}, u32[]{:S(2)}) copy-start(s32[3]{0:T(128)} %pad_add_fusion.tag_ref) | copy-start | bytes 40
  92.9 36.8 %copy-start.1 = (f32[768,640]{1,0:T(8,128)S(1)}, f32[768,640]{1,0:T(8,128)}, u32[]{:S(2)}) copy-start(f32[768,640]{1,0:T(8,128)} %get-tuple-element.42.k_own.v_own) | copy-start | bytes 5898244
  92.9 36.8 %collective-permute-start.5 = (bf16[768,640]{1,0:T(8,128)(2,1)}, bf16[768,640]{1,0:T(8,128)(2,1)}, u32[]{:S(2)}, u32[]{:S(2)}) collective-permute-start(bf16[768,640]{1,0:T(8,128)(2,1)} %add_convert_fusion), channel_id=1, source_target_pairs={{64,0},{96,32},{128,64},{160,96},{192,128},{224,160},{256,192},{28... | collective-permute-start | bytes 2949128 | tf_op jit(solution)/shard_map/ppermute | solution.py:368
  115.2 13.8 %all-to-all-start.4 = ((f32[4,1,1280]{2,1,0:T(1,128)}), f32[4,1,1280]{2,1,0:T(1,128)S(1)}, u32[]{:S(2)}, u32[]{:S(2)}) async-start(f32[4,1,1280]{2,1,0:T(1,128)} %get-tuple-element.46), calls=%async_computation.4 | async-start | bytes 40960 | tf_op jit(solution)/shard_map/all_to_all | solution.py:371
  121.3 1.0 copy-start.2
  122.3 1.2 copy-start.3

commit v3 on v2

--- a/solution.py
+++ b/solution.py
@@ -67,6 +67,7 @@
     slots = q_ref.shape[1]
     width = total_heads * HD
     scale = 1.0 / math.sqrt(HD)
+    steep = scale / math.log(2.0)
     mine = tag_ref[0]
     even = lax.rem(mine, 2) == 0
     distances = (0, 2, jnp.where(even, 3, 1), jnp.where(even, 1, 3))
@@ -118,7 +119,7 @@
         base = slot * slots + at
         included = lanes < limits[slot] - at
         score = jnp.where(included, score_ref[base : base + STRIP, :], MASKED)
-        exponent = jnp.exp((score - top) * scale)
+        exponent = jnp.exp2((score - top) * steep)
         score_ref[base : base + STRIP, :] = exponent
         total += folded(exponent, jnp.add)
         delta += folded(exponent * grad_ref[base : base + STRIP, :], jnp.add)
@@ -411,6 +412,7 @@
         tags, notes, gain_k, inners, k_proj,
         own_part, own_part, side_back, side_back, near_back, near_back,
     )
+    gains, key_grad = lax.optimization_barrier((gains, key_grad))
     gain_sum = jnp.sum(gains[:, 0], axis=0)
     return query_grad, key_grad, value_grad, gain_sum[:local_width], gain_sum[local_width:]
 

time: 135 us -> 131 us (0.970)
  the two profiles are of different devices: /device:TPU:8 before, /device:TPU:40 now
where the time goes in v3:
time: 131 us; the launch traced here: 130 us
  starting transfers between devices  39 us (30%)
  blocking collectives  33.4 us (25%)
  Pallas kernels  29.2 us (22%)
  waiting for transfers between devices  14.9 us (11%)
  other arithmetic  5.83 us (4%)
  local copies, waits for them, and re-layouts  5.59 us (4%)
  between operations  2.15 us (2%)
    pallas_call x1, Pallas kernels, attend(): pl.pallas_call(functools.partial(head_kernel, first, last, heads, len(sta...  18.7 us
    all_to_all x1, blocking collectives, on_device(): inners = lax.all_to_all(inners, 'mp', 0, 0, tiled=True)  17.9 us
    all_to_all x1, blocking collectives, on_device(): rows = lax.all_to_all(rows, 'tm', 0, 0, tiled=True)  15.4 us
    all_to_all x1, starting transfers between devices, on_device(): powers = lax.all_to_all(power, 'mp', 0, 0, tiled=True)  10.3 us
    all_to_all x1, starting transfers between devices, on_device(): gains = lax.all_to_all(gains, 'dp', 0, 0, tiled=True)  7.2 us
    all_to_all x1, waiting for transfers between devices, on_device(): notes = lax.all_to_all(note, 'tm', 0, 0, tiled=True)  7.03 us
    all_to_all x1, starting transfers between devices, on_device(): notes = lax.all_to_all(note, 'tm', 0, 0, tiled=True)  6.09 us
    all_to_all x1, waiting for transfers between devices, on_device(): powers = lax.all_to_all(power, 'mp', 0, 0, tiled=True)  5.93 us
  transfers between devices with their start and end apart: 9, of which 3 were waited for; matrix products, arithmetic and copies ran while one was open for 1% of the time, Pallas kernels for 8%

profile of v3, /device:TPU:40, one launch (start us, length us, event | category | flops | bytes accessed | tf_op | source)
XLA Modules:
  0.0 130.1 jit_solution(9438013100795519181)
XLA Ops:
  0.6 0.0 copy-start
  0.6 0.0 copy-start.10
  0.7 1.3 %pad_maximum_fusion.own_ref = bf16[768,640]{1,0:T(8,128)(2,1)S(1)} fusion(bf16[384,640]{1,0:T(8,128)(2,1)} %bitcast.9, bf16[384,640]{1,0:T(8,128)(2,1)} %bitcast.7), kind=kLoop, calls=%fused_computation.1 | loop fusion | flops 1966080 | bytes 1966080 | tf_op jit(solution)/shard_map/concatenate | solution.py:333
  2.0 0.0 copy-start.15
  2.0 0.0 copy-start.16
  2.0 3.5 %collective-permute-start = (bf16[768,640]{1,0:T(8,128)(2,1)S(1)}, bf16[768,640]{1,0:T(8,128)(2,1)S(1)}, u32[]{:S(2)}, u32[]{:S(2)}) collective-permute-start(bf16[768,640]{1,0:T(8,128)(2,1)S(1)} %pad_maximum_fusion.own_ref), channel_id=1, source_target_pairs={{0,64},{32,96},{64,128},{96,160},{128,192},{160,224},{192,256},{22... | collective-permute-start | bytes 2949128 | tf_op jit(solution)/shard_map/ppermute | solution.py:334
  5.6 2.1 %shard_map.119 = f32[8,1,768]{2,1,0:T(1,128)} custom-call(bf16[1,384,640]{2,1,0:T(8,128)(2,1)} %q_ref.5, bf16[1,384,640]{2,1,0:T(8,128)(2,1)} %k_ref.3), custom_call_target="tpu_custom_call" | custom-call | flops 1000000 | bytes 1000000 | tf_op jit(solution)/shard_map/pallas_call | solution.py:335
  7.6 10.3 %all-to-all-start = ((f32[8,1,768]{2,1,0:T(1,128)}), f32[8,1,768]{2,1,0:T(1,128)S(1)}, u32[]{:S(2)}, u32[]{:S(2)}) async-start(f32[8,1,768]{2,1,0:T(1,128)} %shard_map.119), calls=%async_computation | async-start | bytes 49152 | tf_op jit(solution)/shard_map/all_to_all | solution.py:341
  19.2 0.6 pad_add_fusion.tag_ref
  19.8 5.9 %all-to-all-done.power_ref = f32[8,1,768]{2,1,0:T(1,128)S(1)} async-done(((f32[8,1,768]{2,1,0:T(1,128)}), f32[8,1,768]{2,1,0:T(1,128)S(1)}, u32[]{:S(2)}, u32[]{:S(2)}) %all-to-all-start) | async-done | bytes 24608 | tf_op jit(solution)/shard_map/all_to_all | solution.py:341
  25.8 0.6 copy-done.13
  26.4 1.4 %shard_map.120 = (f32[16,1,512]{2,1,0:T(1,128)}, f32[1,384]{1,0:T(1,128)}) custom-call(s32[3]{0:T(128)} %pad_add_fusion.tag_ref, f32[8,1,768]{2,1,0:T(1,128)} %copy-done.13), custom_call_target="tpu_custom_call" | custom-call | tf_op jit(solution)/shard_map/pallas_call | solution.py:342
  27.8 1.9 %collective-permute-done.near_ref = bf16[768,640]{1,0:T(8,128)(2,1)S(1)} collective-permute-done((bf16[768,640]{1,0:T(8,128)(2,1)S(1)}, bf16[768,640]{1,0:T(8,128)(2,1)S(1)}, u32[]{:S(2)}, u32[]{:S(2)}) %collective-permute-start) | collective-permute-done | bytes 983072 | tf_op jit(solution)/shard_map/ppermute | solution.py:334
  29.7 0.0 copy-done.10
  29.7 1.2 broadcast_select_fusion
  30.9 0.0 copy-done.11
  30.9 1.9 %collective-permute-start.1 = (bf16[768,640]{1,0:T(8,128)(2,1)}, bf16[768,640]{1,0:T(8,128)(2,1)}, u32[]{:S(2)}, u32[]{:S(2)}) collective-permute-start(bf16[768,640]{1,0:T(8,128)(2,1)} %broadcast_select_fusion), channel_id=1, source_target_pairs={{0,32},{32,64},{64,96},{96,128},{128,160},{160,192},{192,224},{224... | collective-permute-start | bytes 2949128 | tf_op jit(solution)/shard_map/ppermute | solution.py:350
  32.8 1.9 %collective-permute-start.2 = (bf16[768,640]{1,0:T(8,128)(2,1)S(1)}, bf16[768,640]{1,0:T(8,128)(2,1)S(1)}, u32[]{:S(2)}, u32[]{:S(2)}) collective-permute-start(bf16[768,640]{1,0:T(8,128)(2,1)S(1)} %collective-permute-done.near_ref), channel_id=1, source_target_pairs={{0,32},{32,0},{64,96},{96,64},{128,160},{160,128},{192,224},{224,1... | collective-permute-start | bytes 2949128 | tf_op jit(solution)/shard_map/ppermute | solution.py:351
  34.8 6.1 %all-to-all-start.1 = ((f32[16,1,512]{2,1,0:T(1,128)}), f32[16,1,512]{2,1,0:T(1,128)S(1)}, u32[]{:S(2)}, u32[]{:S(2)}) async-start(f32[16,1,512]{2,1,0:T(1,128)} %get-tuple-element.32), calls=%async_computation.1 | async-start | bytes 65536 | tf_op jit(solution)/shard_map/all_to_all | solution.py:352
  40.9 0.6 reshape.16.gain_q_ref.gain_ref
  41.4 0.6 reshape.17.gain_k_ref.gain_ref
  42.0 7.0 %all-to-all-done.1.notes = f32[16,1,512]{2,1,0:T(1,128)S(1)} async-done(((f32[16,1,512]{2,1,0:T(1,128)}), f32[16,1,512]{2,1,0:T(1,128)S(1)}, u32[]{:S(2)}, u32[]{:S(2)}) %all-to-all-start.1) | async-done | bytes 32800 | tf_op jit(solution)/shard_map/all_to_all | solution.py:352
  49.1 0.0 collective-permute-done.1.side_ref
  49.1 0.0 collective-permute-done.2.swap_ref
  49.1 0.6 copy-done.4
  49.7 0.3 copy-done.17
  50.0 18.7 %shard_map.121 = (f32[384,640]{1,0:T(8,128)}, f32[768,640]{1,0:T(8,128)}, bf16[768,640]{1,0:T(8,128)(2,1)}, bf16[768,640]{1,0:T(8,128)(2,1)}, bf16[768,640]{1,0:...) custom-call(s32[3]{0:T(128)} %pad_add_fusion.tag_ref, f32[16,1,512]{2,1,0:T(1,128)} %copy-done.4, ...), custom_call_target="tpu_custom_call" | custom-call | flops 3774873600 | bytes 10813440 | tf_op jit(solution)/shard_map/pallas_call | solution.py:192
  68.8 2.0 %collective-permute-start.3 = (bf16[768,640]{1,0:T(8,128)(2,1)}, bf16[768,640]{1,0:T(8,128)(2,1)S(1)}, u32[]{:S(2)}, u32[]{:S(2)}) collective-permute-start(bf16[768,640]{1,0:T(8,128)(2,1)} %get-tuple-element.39), channel_id=1, source_target_pairs={{0,32},{32,0},{64,96},{96,64},{128,160},{160,128},{192,224},{224,1... | collective-permute-start | bytes 2949128 | tf_op jit(solution)/shard_map/ppermute | solution.py:359
  70.7 1.9 %collective-permute-start.4 = (bf16[768,640]{1,0:T(8,128)(2,1)}, bf16[768,640]{1,0:T(8,128)(2,1)S(1)}, u32[]{:S(2)}, u32[]{:S(2)}) collective-permute-start(bf16[768,640]{1,0:T(8,128)(2,1)} %get-tuple-element.40), channel_id=1, source_target_pairs={{32,0},{64,32},{96,64},{128,96},{160,128},{192,160},{224,192},{256... | collective-permute-start | bytes 2949128 | tf_op jit(solution)/shard_map/ppermute | solution.py:358
  72.7 15.4 %all_to_all.25.rows_ref = f32[16,1,1664]{2,1,0:T(1,128)} all-to-all(f32[16,1,1664]{2,1,0:T(1,128)} %get-tuple-element.35), channel_id=1, replica_groups=mesh['tm'=16,'mp'=8,'dp'=4] {'tm'}, dimensions={0} | all-to-all | bytes 212992 | tf_op jit(solution)/shard_map/all_to_all | solution.py:360
  88.1 1.5 %shard_map.122 = (f32[8,1,768]{2,1,0:T(1,128)}, f32[4,1,1280]{2,1,0:T(1,128)}) custom-call(f32[8,1280]{1,0:T(8,128)} %get-tuple-element.34.state_ref, f32[16,1,1664]{2,1,0:T(1,128)} %all_to_all.25.rows_ref), custom_call_target="tpu_custom_call" | custom-call | tf_op jit(solution)/shard_map/pallas_call | solution.py:361
  89.6 0.0 collective-permute-done.3
  89.6 0.0 collective-permute-done.4.k_side.v_side
  89.6 0.0 copy-start.14
  89.7 0.0 copy-start.6
  89.7 0.0 copy-start.9
  89.7 0.0 copy-start.7
  89.7 2.6 %add_convert_fusion = bf16[768,640]{1,0:T(8,128)(2,1)} fusion(bf16[768,640]{1,0:T(8,128)(2,1)S(1)} %collective-permute-done.4.k_side.v_side, bf16[768,640]{1,0:T(8,128)(2,1)S(1)} %collective-permute-done.3, bf16[768,640]{1,0:T(8,128)(2,1)} %get-tuple-element.38, pred[]{:T(512)S(6)} %eq.5), kind=kLoop, calls=%fused_computation | loop fusion | flops 3440640 | bytes 3932161 | tf_op jit(solution)/shard_map/convert_element_type | solution.py:367
  92.3 4.2 %collective-permute-start.5 = (bf16[768,640]{1,0:T(8,128)(2,1)}, bf16[768,640]{1,0:T(8,128)(2,1)}, u32[]{:S(2)}, u32[]{:S(2)}) collective-permute-start(bf16[768,640]{1,0:T(8,128)(2,1)} %add_convert_fusion), channel_id=1, source_target_pairs={{64,0},{96,32},{128,64},{160,96},{192,128},{224,160},{256,192},{28... | collective-permute-start | bytes 2949128 | tf_op jit(solution)/shard_map/ppermute | solution.py:369
  96.5 17.9 %all_to_all.26.inners = f32[8,1,768]{2,1,0:T(1,128)S(1)} all-to-all(f32[8,1,768]{2,1,0:T(1,128)S(1)} %copy-done.14), channel_id=1, replica_groups=mesh['tm'=16,'mp'=8,'dp'=4] {'mp'}, dimensions={0} | all-to-all | bytes 49152 | tf_op jit(solution)/shard_map/all_to_all | solution.py:370
  114.5 7.2 %all-to-all-start.4 = ((f32[4,1,1280]{2,1,0:T(1,128)}), f32[4,1,1280]{2,1,0:T(1,128)S(1)}, u32[]{:S(2)}, u32[]{:S(2)}) async-start(f32[4,1,1280]{2,1,0:T(1,128)} %get-tuple-element.44), calls=%async_computation.4 | async-start | bytes 40960 | tf_op jit(solution)/shard_map/all_to_all | solution.py:372
  121.7 1.0 copy-done.2
  122.7 1.2 copy-done.3
  123.9 1.6 %shard_map.123 = bf16[1,384,640]{2,1,0:T(8,128)(2,1)} custom-call(f32[1,384]{1,0:T(1,128)S(1)} %copy-done.9, f32[1,640]{1,0:T(1,128)S(1)} %copy-done.6, f32[8,1,768]{2,1,0:T(1,128)S(1)} %all_to_all.26.inners, bf16[1,384,640]{2,1,0:T(8,128)(2,1)S(1)} %copy-done.2, f32[384,640]{1,0:T(8,128)S(1)} %copy-done.3), custom_call_target="tpu_custom_call" | custom-call | flops 1000000 | bytes 3000000 | tf_op jit(solution)/shard_map/pallas_call | solution.py:379
  125.6 0.0 collective-permute-done.5.k_near.v_near
  125.6 3.8 %shard_map.124 = (bf16[1,384,640]{2,1,0:T(8,128)(2,1)}, bf16[1,384,640]{2,1,0:T(8,128)(2,1)}) custom-call(s32[3]{0:T(128)S(1)} %copy-done.8, f32[16,1,512]{2,1,0:T(1,128)S(1)} %copy-done.5, f32[1,640]{1,0:T(1,128)S(1)} %copy-done.7, f32[8,1,768]{2,1,0:T(1,128)S(1)} %all_to_all.26.inners, bf16[1,384,640]{2,1,0:T(8,128)(2,1)S(1)} %copy-done, ...), custom_call_target="tpu_custom_call" | custom-call | flops 1000000 | bytes 5000000 | tf_op jit(solution)/shard_map/pallas_call | solution.py:395
  129.4 0.0 all-to-all-done.4
  129.5 0.6 fusion
  (22 shorter events, 0.1 us)
Async XLA Ops:
  0.6 29.0 %copy-start = (bf16[1,384,640]{2,1,0:T(8,128)(2,1)S(1)}, bf16[1,384,640]{2,1,0:T(8,128)(2,1)}, u32[]{:S(2)}) copy-start(bf16[1,384,640]{2,1,0:T(8,128)(2,1)} %k_ref.3) | copy-start | bytes 1474564
  0.6 29.0 %copy-start.10 = (bf16[1,384,640]{2,1,0:T(8,128)(2,1)S(1)}, bf16[1,384,640]{2,1,0:T(8,128)(2,1)}, u32[]{:S(2)}) copy-start(bf16[1,384,640]{2,1,0:T(8,128)(2,1)} %param.10) | copy-start | bytes 1474564
  2.0 28.9 %copy-start.11 = (bf16[768,640]{1,0:T(8,128)(2,1)}, bf16[768,640]{1,0:T(8,128)(2,1)S(1)}, u32[]{:S(2)}) copy-start(bf16[768,640]{1,0:T(8,128)(2,1)S(1)} %pad_maximum_fusion.own_ref) | copy-start | bytes 2949124
  2.0 38.8 %copy-start.15 = (f32[640]{0:T(1024)S(1)}, f32[640]{0:T(1024)}, u32[]{:S(2)}) copy-start(f32[640]{0:T(1024)} %param.12) | copy-start | bytes 7684
  2.0 39.4 %copy-start.16 = (f32[640]{0:T(1024)S(1)}, f32[640]{0:T(1024)}, u32[]{:S(2)}) copy-start(f32[640]{0:T(1024)} %param.13) | copy-start | bytes 7684
  2.0 27.6 %collective-permute-start = (bf16[768,640]{1,0:T(8,128)(2,1)S(1)}, bf16[768,640]{1,0:T(8,128)(2,1)S(1)}, u32[]{:S(2)}, u32[]{:S(2)}) collective-permute-start(bf16[768,640]{1,0:T(8,128)(2,1)S(1)} %pad_maximum_fusion.own_ref), channel_id=1, source_target_pairs={{0,64},{32,96},{64,128},{96,160},{128,192},{160,224},{192,256},{22... | collective-permute-start | bytes 2949128 | tf_op jit(solution)/shard_map/ppermute | solution.py:334
  7.6 18.1 %all-to-all-start = ((f32[8,1,768]{2,1,0:T(1,128)}), f32[8,1,768]{2,1,0:T(1,128)S(1)}, u32[]{:S(2)}, u32[]{:S(2)}) async-start(f32[8,1,768]{2,1,0:T(1,128)} %shard_map.119), calls=%async_computation | async-start | bytes 49152 | tf_op jit(solution)/shard_map/all_to_all | solution.py:341
  25.8 0.6 copy-start.13
  29.7 19.4 %copy-start.12 = (bf16[768,640]{1,0:T(8,128)(2,1)}, bf16[768,640]{1,0:T(8,128)(2,1)S(1)}, u32[]{:S(2)}) copy-start(bf16[768,640]{1,0:T(8,128)(2,1)S(1)} %collective-permute-done.near_ref) | copy-start | bytes 2949124
  30.9 18.1 %collective-permute-start.1 = (bf16[768,640]{1,0:T(8,128)(2,1)}, bf16[768,640]{1,0:T(8,128)(2,1)}, u32[]{:S(2)}, u32[]{:S(2)}) collective-permute-start(bf16[768,640]{1,0:T(8,128)(2,1)} %broadcast_select_fusion), channel_id=1, source_target_pairs={{0,32},{32,64},{64,96},{96,128},{128,160},{160,192},{192,224},{224... | collective-permute-start | bytes 2949128 | tf_op jit(solution)/shard_map/ppermute | solution.py:350
  32.8 16.2 %collective-permute-start.2 = (bf16[768,640]{1,0:T(8,128)(2,1)S(1)}, bf16[768,640]{1,0:T(8,128)(2,1)S(1)}, u32[]{:S(2)}, u32[]{:S(2)}) collective-permute-start(bf16[768,640]{1,0:T(8,128)(2,1)S(1)} %collective-permute-done.near_ref), channel_id=1, source_target_pairs={{0,32},{32,0},{64,96},{96,64},{128,160},{160,128},{192,224},{224,1... | collective-permute-start | bytes 2949128 | tf_op jit(solution)/shard_map/ppermute | solution.py:351
  34.8 14.3 %all-to-all-start.1 = ((f32[16,1,512]{2,1,0:T(1,128)}), f32[16,1,512]{2,1,0:T(1,128)S(1)}, u32[]{:S(2)}, u32[]{:S(2)}) async-start(f32[16,1,512]{2,1,0:T(1,128)} %get-tuple-element.32), calls=%async_computation.1 | async-start | bytes 65536 | tf_op jit(solution)/shard_map/all_to_all | solution.py:352
  49.1 0.6 copy-start.4
  49.1 0.9 copy-start.17
  68.8 20.9 %collective-permute-start.3 = (bf16[768,640]{1,0:T(8,128)(2,1)}, bf16[768,640]{1,0:T(8,128)(2,1)S(1)}, u32[]{:S(2)}, u32[]{:S(2)}) collective-permute-start(bf16[768,640]{1,0:T(8,128)(2,1)} %get-tuple-element.39), channel_id=1, source_target_pairs={{0,32},{32,0},{64,96},{96,64},{128,160},{160,128},{192,224},{224,1... | collective-permute-start | bytes 2949128 | tf_op jit(solution)/shard_map/ppermute | solution.py:359
  70.7 18.9 %collective-permute-start.4 = (bf16[768,640]{1,0:T(8,128)(2,1)}, bf16[768,640]{1,0:T(8,128)(2,1)S(1)}, u32[]{:S(2)}, u32[]{:S(2)}) collective-permute-start(bf16[768,640]{1,0:T(8,128)(2,1)} %get-tuple-element.40), channel_id=1, source_target_pairs={{32,0},{64,32},{96,64},{128,96},{160,128},{192,160},{224,192},{256... | collective-permute-start | bytes 2949128 | tf_op jit(solution)/shard_map/ppermute | solution.py:358
  89.6 6.9 %copy-start.14 = (f32[8,1,768]{2,1,0:T(1,128)S(1)}, f32[8,1,768]{2,1,0:T(1,128)}, u32[]{:S(2)}) copy-start(f32[8,1,768]{2,1,0:T(1,128)} %get-tuple-element.41) | copy-start | bytes 73732
  89.7 32.0 %copy-start.6 = (f32[1,640]{1,0:T(1,128)S(1)}, f32[1,640]{1,0:T(1,128)}, u32[]{:S(2)}) copy-start(f32[1,640]{1,0:T(1,128)} %reshape.16.gain_q_ref.gain_ref) | copy-start | bytes 7684
  89.7 32.0 %copy-start.9 = (f32[1,384]{1,0:T(1,128)S(1)}, f32[1,384]{1,0:T(1,128)}, u32[]{:S(2)}) copy-start(f32[1,384]{1,0:T(1,128)} %get-tuple-element.28.q_inverse) | copy-start | bytes 4612
  89.7 35.9 %copy-start.5 = (f32[16,1,512]{2,1,0:T(1,128)S(1)}, f32[16,1,512]{2,1,0:T(1,128)}, u32[]{:S(2)}) copy-start(f32[16,1,512]{2,1,0:T(1,128)} %copy-done.4) | copy-start | bytes 98308
  89.7 35.9 %copy-start.7 = (f32[1,640]{1,0:T(1,128)S(1)}, f32[1,640]{1,0:T(1,128)}, u32[]{:S(2)}) copy-start(f32[1,640]{1,0:T(1,128)} %reshape.17.gain_k_ref.gain_ref) | copy-start | bytes 7684
  89.7 35.9 %copy-start.8 = (s32[3]{0:T(128)S(1)}, s32[3]{0:T(128)}, u32[]{:S(2)}) copy-start(s32[3]{0:T(128)} %pad_add_fusion.tag_ref) | copy-start | bytes 40
  92.3 33.2 %copy-start.1 = (f32[768,640]{1,0:T(8,128)S(1)}, f32[768,640]{1,0:T(8,128)}, u32[]{:S(2)}) copy-start(f32[768,640]{1,0:T(8,128)} %get-tuple-element.45.k_own.v_own) | copy-start | bytes 5898244
  92.3 33.2 %collective-permute-start.5 = (bf16[768,640]{1,0:T(8,128)(2,1)}, bf16[768,640]{1,0:T(8,128)(2,1)}, u32[]{:S(2)}, u32[]{:S(2)}) collective-permute-start(bf16[768,640]{1,0:T(8,128)(2,1)} %add_convert_fusion), channel_id=1, source_target_pairs={{64,0},{96,32},{128,64},{160,96},{192,128},{224,160},{256,192},{28... | collective-permute-start | bytes 2949128 | tf_op jit(solution)/shard_map/ppermute | solution.py:369
  114.5 15.0 %all-to-all-start.4 = ((f32[4,1,1280]{2,1,0:T(1,128)}), f32[4,1,1280]{2,1,0:T(1,128)S(1)}, u32[]{:S(2)}, u32[]{:S(2)}) async-start(f32[4,1,1280]{2,1,0:T(1,128)} %get-tuple-element.44), calls=%async_computation.4 | async-start | bytes 40960 | tf_op jit(solution)/shard_map/all_to_all | solution.py:372
  121.7 1.0 copy-start.2
  122.7 1.2 copy-start.3

commit v4 on v3

--- a/solution.py
+++ b/solution.py
@@ -389,7 +389,7 @@
         out_specs=raw,
         out_shape=struct(q_proj.shape, LOW),
         scratch_shapes=[pltpu.VMEM((2, slots, HD), F32)],
-        compiler_params=kernel_params(16 * 1024 * 1024),
+        compiler_params=kernel_params(),
         cost_estimate=pl.CostEstimate(flops=10**6, bytes_accessed=3 * 10**6, transcendentals=0),
     )(q_inverse, gain_q, inners, q_proj, q_part)
     key_grad, value_grad = pl.pallas_call(

time: 131 us -> 131 us (level)
  local copies, waits for them, and re-layouts: 5.59 us -> 3.34 us
  Pallas kernels: 29.2 us -> 31.2 us
    unnamed x36 -> x30, local copies, waits for them, and re-layouts: 3.83 us -> 1.58 us
    pallas_call x1, Pallas kernels: 1.65 us -> 3.62 us  [on_device(): pl.pallas_call(functools.partial(query_kernel, full_width), grid=(steps,)...]
  transfers between devices with their start and end apart: 9 -> 9, of which waited for: 3 -> 3; matrix products, arithmetic and copies ran while one was open for 1% -> 1% of each run, Pallas kernels for 8% -> 10%
where the time goes in v4:
time: 131 us; the launch traced here: 130 us
  starting transfers between devices  39.2 us (30%)
  blocking collectives  33.5 us (26%)
  Pallas kernels  31.2 us (24%)
  waiting for transfers between devices  14.9 us (11%)
  other arithmetic  5.8 us (4%)
  local copies, waits for them, and re-layouts  3.34 us (3%)
  between operations  2.12 us (2%)
    pallas_call x1, Pallas kernels, attend(): pl.pallas_call(functools.partial(head_kernel, first, last, heads, len(sta...  18.7 us
    all_to_all x1, blocking collectives, on_device(): inners = lax.all_to_all(inners, 'mp', 0, 0, tiled=True)  18 us
    all_to_all x1, blocking collectives, on_device(): rows = lax.all_to_all(rows, 'tm', 0, 0, tiled=True)  15.4 us
    all_to_all x1, starting transfers between devices, on_device(): powers = lax.all_to_all(power, 'mp', 0, 0, tiled=True)  10.3 us
    all_to_all x1, starting transfers between devices, on_device(): gains = lax.all_to_all(gains, 'dp', 0, 0, tiled=True)  7.33 us
    all_to_all x1, waiting for transfers between devices, on_device(): notes = lax.all_to_all(note, 'tm', 0, 0, tiled=True)  7.03 us
    all_to_all x1, starting transfers between devices, on_device(): notes = lax.all_to_all(note, 'tm', 0, 0, tiled=True)  6.09 us
    all_to_all x1, waiting for transfers between devices, on_device(): powers = lax.all_to_all(power, 'mp', 0, 0, tiled=True)  5.94 us
  transfers between devices with their start and end apart: 9, of which 3 were waited for; matrix products, arithmetic and copies ran while one was open for 1% of the time, Pallas kernels for 10%

profile of v4, /device:TPU:40, one launch (start us, length us, event | category | flops | bytes accessed | tf_op | source)
XLA Modules:
  0.0 130.0 jit_solution(15741620440429243664)
XLA Ops:
  0.6 0.0 copy-start
  0.6 0.0 copy-start.7
  0.7 1.3 %pad_maximum_fusion.own_ref = bf16[768,640]{1,0:T(8,128)(2,1)S(1)} fusion(bf16[384,640]{1,0:T(8,128)(2,1)} %bitcast.9, bf16[384,640]{1,0:T(8,128)(2,1)} %bitcast.7), kind=kLoop, calls=%fused_computation.1 | loop fusion | flops 1966080 | bytes 1966080 | tf_op jit(solution)/shard_map/concatenate | solution.py:333
  2.0 0.0 copy-start.8
  2.0 0.0 copy-start.12
  2.0 0.0 copy-start.13
  2.0 3.5 %collective-permute-start = (bf16[768,640]{1,0:T(8,128)(2,1)S(1)}, bf16[768,640]{1,0:T(8,128)(2,1)S(1)}, u32[]{:S(2)}, u32[]{:S(2)}) collective-permute-start(bf16[768,640]{1,0:T(8,128)(2,1)S(1)} %pad_maximum_fusion.own_ref), channel_id=1, source_target_pairs={{0,64},{32,96},{64,128},{96,160},{128,192},{160,224},{192,256},{22... | collective-permute-start | bytes 2949128 | tf_op jit(solution)/shard_map/ppermute | solution.py:334
  5.6 2.1 %shard_map.119 = f32[8,1,768]{2,1,0:T(1,128)} custom-call(bf16[1,384,640]{2,1,0:T(8,128)(2,1)} %q_ref.5, bf16[1,384,640]{2,1,0:T(8,128)(2,1)} %k_ref.3), custom_call_target="tpu_custom_call" | custom-call | flops 1000000 | bytes 1000000 | tf_op jit(solution)/shard_map/pallas_call | solution.py:335
  7.6 10.3 %all-to-all-start = ((f32[8,1,768]{2,1,0:T(1,128)}), f32[8,1,768]{2,1,0:T(1,128)S(1)}, u32[]{:S(2)}, u32[]{:S(2)}) async-start(f32[8,1,768]{2,1,0:T(1,128)} %shard_map.119), calls=%async_computation | async-start | bytes 49152 | tf_op jit(solution)/shard_map/all_to_all | solution.py:341
  19.2 0.6 pad_add_fusion.tag_ref
  19.8 5.9 %all-to-all-done.power_ref = f32[8,1,768]{2,1,0:T(1,128)S(1)} async-done(((f32[8,1,768]{2,1,0:T(1,128)}), f32[8,1,768]{2,1,0:T(1,128)S(1)}, u32[]{:S(2)}, u32[]{:S(2)}) %all-to-all-start) | async-done | bytes 24608 | tf_op jit(solution)/shard_map/all_to_all | solution.py:341
  25.8 0.6 copy-done.10
  26.4 1.4 %shard_map.120 = (f32[16,1,512]{2,1,0:T(1,128)}, f32[1,384]{1,0:T(1,128)}) custom-call(s32[3]{0:T(128)} %pad_add_fusion.tag_ref, f32[8,1,768]{2,1,0:T(1,128)} %copy-done.10), custom_call_target="tpu_custom_call" | custom-call | tf_op jit(solution)/shard_map/pallas_call | solution.py:342
  27.8 1.9 %collective-permute-done.near_ref = bf16[768,640]{1,0:T(8,128)(2,1)S(1)} collective-permute-done((bf16[768,640]{1,0:T(8,128)(2,1)S(1)}, bf16[768,640]{1,0:T(8,128)(2,1)S(1)}, u32[]{:S(2)}, u32[]{:S(2)}) %collective-permute-start) | collective-permute-done | bytes 983072 | tf_op jit(solution)/shard_map/ppermute | solution.py:334
  29.7 0.0 copy-done
  29.7 0.0 copy-done.7
  29.7 1.2 broadcast_select_fusion
  30.9 0.0 copy-done.8
  30.9 1.9 %collective-permute-start.1 = (bf16[768,640]{1,0:T(8,128)(2,1)}, bf16[768,640]{1,0:T(8,128)(2,1)}, u32[]{:S(2)}, u32[]{:S(2)}) collective-permute-start(bf16[768,640]{1,0:T(8,128)(2,1)} %broadcast_select_fusion), channel_id=1, source_target_pairs={{0,32},{32,64},{64,96},{96,128},{128,160},{160,192},{192,224},{224... | collective-permute-start | bytes 2949128 | tf_op jit(solution)/shard_map/ppermute | solution.py:350
  32.8 1.9 %collective-permute-start.2 = (bf16[768,640]{1,0:T(8,128)(2,1)S(1)}, bf16[768,640]{1,0:T(8,128)(2,1)S(1)}, u32[]{:S(2)}, u32[]{:S(2)}) collective-permute-start(bf16[768,640]{1,0:T(8,128)(2,1)S(1)} %collective-permute-done.near_ref), channel_id=1, source_target_pairs={{0,32},{32,0},{64,96},{96,64},{128,160},{160,128},{192,224},{224,1... | collective-permute-start | bytes 2949128 | tf_op jit(solution)/shard_map/ppermute | solution.py:351
  34.8 6.1 %all-to-all-start.1 = ((f32[16,1,512]{2,1,0:T(1,128)}), f32[16,1,512]{2,1,0:T(1,128)S(1)}, u32[]{:S(2)}, u32[]{:S(2)}) async-start(f32[16,1,512]{2,1,0:T(1,128)} %get-tuple-element.32), calls=%async_computation.1 | async-start | bytes 65536 | tf_op jit(solution)/shard_map/all_to_all | solution.py:352
  40.9 0.0 copy-done.12
  40.9 0.6 reshape.16.gain_q_ref.gain_ref
  41.4 0.0 copy-done.13
  41.4 0.6 reshape.17.gain_k_ref.gain_ref
  42.0 7.0 %all-to-all-done.1.notes = f32[16,1,512]{2,1,0:T(1,128)S(1)} async-done(((f32[16,1,512]{2,1,0:T(1,128)}), f32[16,1,512]{2,1,0:T(1,128)S(1)}, u32[]{:S(2)}, u32[]{:S(2)}) %all-to-all-start.1) | async-done | bytes 32800 | tf_op jit(solution)/shard_map/all_to_all | solution.py:352
  49.1 0.0 collective-permute-done.1.side_ref
  49.1 0.0 collective-permute-done.2.swap_ref
  49.1 0.6 copy-done.3
  49.7 0.3 copy-done.14
  50.0 18.7 %shard_map.121 = (f32[384,640]{1,0:T(8,128)}, f32[768,640]{1,0:T(8,128)}, bf16[768,640]{1,0:T(8,128)(2,1)}, bf16[768,640]{1,0:T(8,128)(2,1)}, bf16[768,640]{1,0:...) custom-call(s32[3]{0:T(128)} %pad_add_fusion.tag_ref, f32[16,1,512]{2,1,0:T(1,128)} %copy-done.3, ...), custom_call_target="tpu_custom_call" | custom-call | flops 3774873600 | bytes 10813440 | tf_op jit(solution)/shard_map/pallas_call | solution.py:192
  68.7 2.0 %collective-permute-start.3 = (bf16[768,640]{1,0:T(8,128)(2,1)}, bf16[768,640]{1,0:T(8,128)(2,1)S(1)}, u32[]{:S(2)}, u32[]{:S(2)}) collective-permute-start(bf16[768,640]{1,0:T(8,128)(2,1)} %get-tuple-element.39), channel_id=1, source_target_pairs={{0,32},{32,0},{64,96},{96,64},{128,160},{160,128},{192,224},{224,1... | collective-permute-start | bytes 2949128 | tf_op jit(solution)/shard_map/ppermute | solution.py:359
  70.7 1.9 %collective-permute-start.4 = (bf16[768,640]{1,0:T(8,128)(2,1)}, bf16[768,640]{1,0:T(8,128)(2,1)S(1)}, u32[]{:S(2)}, u32[]{:S(2)}) collective-permute-start(bf16[768,640]{1,0:T(8,128)(2,1)} %get-tuple-element.40), channel_id=1, source_target_pairs={{32,0},{64,32},{96,64},{128,96},{160,128},{192,160},{224,192},{256... | collective-permute-start | bytes 2949128 | tf_op jit(solution)/shard_map/ppermute | solution.py:358
  72.6 15.4 %all_to_all.25.rows_ref = f32[16,1,1664]{2,1,0:T(1,128)} all-to-all(f32[16,1,1664]{2,1,0:T(1,128)} %get-tuple-element.35), channel_id=1, replica_groups=mesh['tm'=16,'mp'=8,'dp'=4] {'tm'}, dimensions={0} | all-to-all | bytes 212992 | tf_op jit(solution)/shard_map/all_to_all | solution.py:360
  88.1 1.5 %shard_map.122 = (f32[8,1,768]{2,1,0:T(1,128)}, f32[4,1,1280]{2,1,0:T(1,128)}) custom-call(f32[8,1280]{1,0:T(8,128)} %get-tuple-element.34.state_ref, f32[16,1,1664]{2,1,0:T(1,128)} %all_to_all.25.rows_ref), custom_call_target="tpu_custom_call" | custom-call | tf_op jit(solution)/shard_map/pallas_call | solution.py:361
  89.6 0.0 collective-permute-done.3
  89.6 0.0 collective-permute-done.4.k_side.v_side
  89.6 0.0 copy-start.11
  89.6 2.6 %add_convert_fusion = bf16[768,640]{1,0:T(8,128)(2,1)} fusion(bf16[768,640]{1,0:T(8,128)(2,1)S(1)} %collective-permute-done.4.k_side.v_side, bf16[768,640]{1,0:T(8,128)(2,1)S(1)} %collective-permute-done.3, bf16[768,640]{1,0:T(8,128)(2,1)} %get-tuple-element.38, pred[]{:T(512)S(6)} %eq.5), kind=kLoop, calls=%fused_computation | loop fusion | flops 3440640 | bytes 3932161 | tf_op jit(solution)/shard_map/convert_element_type | solution.py:367
  92.3 4.2 %collective-permute-start.5 = (bf16[768,640]{1,0:T(8,128)(2,1)}, bf16[768,640]{1,0:T(8,128)(2,1)}, u32[]{:S(2)}, u32[]{:S(2)}) collective-permute-start(bf16[768,640]{1,0:T(8,128)(2,1)} %add_convert_fusion), channel_id=1, source_target_pairs={{64,0},{96,32},{128,64},{160,96},{192,128},{224,160},{256,192},{28... | collective-permute-start | bytes 2949128 | tf_op jit(solution)/shard_map/ppermute | solution.py:369
  96.5 18.0 %all_to_all.26.inners = f32[8,1,768]{2,1,0:T(1,128)} all-to-all(f32[8,1,768]{2,1,0:T(1,128)S(1)} %copy-done.11), channel_id=1, replica_groups=mesh['tm'=16,'mp'=8,'dp'=4] {'mp'}, dimensions={0} | all-to-all | bytes 49152 | tf_op jit(solution)/shard_map/all_to_all | solution.py:370
  114.5 7.3 %all-to-all-start.4 = ((f32[4,1,1280]{2,1,0:T(1,128)}), f32[4,1,1280]{2,1,0:T(1,128)S(1)}, u32[]{:S(2)}, u32[]{:S(2)}) async-start(f32[4,1,1280]{2,1,0:T(1,128)} %get-tuple-element.44), calls=%async_computation.4 | async-start | bytes 40960 | tf_op jit(solution)/shard_map/all_to_all | solution.py:372
  121.9 3.6 %shard_map.123 = bf16[1,384,640]{2,1,0:T(8,128)(2,1)} custom-call(f32[1,384]{1,0:T(1,128)} %get-tuple-element.28.q_inverse, f32[1,640]{1,0:T(1,128)} %reshape.16.gain_q_ref.gain_ref, f32[8,1,768]{2,1,0:T(1,128)} %all_to_all.26.inners, bf16[1,384,640]{2,1,0:T(8,128)(2,1)} %q_ref.5, f32[384,640]{1,0:T(8,128)} %get-tuple-element.43.q_part), custom_call_target="tpu_custom_call" | custom-call | flops 1000000 | bytes 3000000 | tf_op jit(solution)/shard_map/pallas_call | solution.py:379
  125.5 0.0 collective-permute-done.5.k_near.v_near
  125.5 0.0 copy-done.1
  125.5 3.8 %shard_map.124 = (bf16[1,384,640]{2,1,0:T(8,128)(2,1)}, bf16[1,384,640]{2,1,0:T(8,128)(2,1)}) custom-call(s32[3]{0:T(128)S(1)} %copy-done.6, f32[16,1,512]{2,1,0:T(1,128)S(1)} %copy-done.4, f32[1,640]{1,0:T(1,128)S(1)} %copy-done.5, f32[8,1,768]{2,1,0:T(1,128)S(1)} %copy-done.2, bf16[1,384,640]{2,1,0:T(8,128)(2,1)S(1)} %copy-done, f32[768,640]{1,0:T(8,128)S(1)} %copy-done.1, ...), custom_call_target="tpu_custom_call" | custom-call | flops 1000000 | bytes 5000000 | tf_op jit(solution)/shard_map/pallas_call | solution.py:395
  129.3 0.0 all-to-all-done.4
  129.4 0.6 fusion
  (16 shorter events, 0.1 us)
Async XLA Ops:
  0.6 29.0 %copy-start = (bf16[1,384,640]{2,1,0:T(8,128)(2,1)S(1)}, bf16[1,384,640]{2,1,0:T(8,128)(2,1)}, u32[]{:S(2)}) copy-start(bf16[1,384,640]{2,1,0:T(8,128)(2,1)} %k_ref.3) | copy-start | bytes 1474564
  0.6 29.0 %copy-start.7 = (bf16[1,384,640]{2,1,0:T(8,128)(2,1)S(1)}, bf16[1,384,640]{2,1,0:T(8,128)(2,1)}, u32[]{:S(2)}) copy-start(bf16[1,384,640]{2,1,0:T(8,128)(2,1)} %param.10) | copy-start | bytes 1474564
  2.0 28.9 %copy-start.8 = (bf16[768,640]{1,0:T(8,128)(2,1)}, bf16[768,640]{1,0:T(8,128)(2,1)S(1)}, u32[]{:S(2)}) copy-start(bf16[768,640]{1,0:T(8,128)(2,1)S(1)} %pad_maximum_fusion.own_ref) | copy-start | bytes 2949124
  2.0 38.8 %copy-start.12 = (f32[640]{0:T(1024)S(1)}, f32[640]{0:T(1024)}, u32[]{:S(2)}) copy-start(f32[640]{0:T(1024)} %param.12) | copy-start | bytes 7684
  2.0 39.4 %copy-start.13 = (f32[640]{0:T(1024)S(1)}, f32[640]{0:T(1024)}, u32[]{:S(2)}) copy-start(f32[640]{0:T(1024)} %param.13) | copy-start | bytes 7684
  2.0 27.6 %collective-permute-start = (bf16[768,640]{1,0:T(8,128)(2,1)S(1)}, bf16[768,640]{1,0:T(8,128)(2,1)S(1)}, u32[]{:S(2)}, u32[]{:S(2)}) collective-permute-start(bf16[768,640]{1,0:T(8,128)(2,1)S(1)} %pad_maximum_fusion.own_ref), channel_id=1, source_target_pairs={{0,64},{32,96},{64,128},{96,160},{128,192},{160,224},{192,256},{22... | collective-permute-start | bytes 2949128 | tf_op jit(solution)/shard_map/ppermute | solution.py:334
  7.6 18.1 %all-to-all-start = ((f32[8,1,768]{2,1,0:T(1,128)}), f32[8,1,768]{2,1,0:T(1,128)S(1)}, u32[]{:S(2)}, u32[]{:S(2)}) async-start(f32[8,1,768]{2,1,0:T(1,128)} %shard_map.119), calls=%async_computation | async-start | bytes 49152 | tf_op jit(solution)/shard_map/all_to_all | solution.py:341
  25.8 0.6 copy-start.10
  29.7 19.4 %copy-start.9 = (bf16[768,640]{1,0:T(8,128)(2,1)}, bf16[768,640]{1,0:T(8,128)(2,1)S(1)}, u32[]{:S(2)}) copy-start(bf16[768,640]{1,0:T(8,128)(2,1)S(1)} %collective-permute-done.near_ref) | copy-start | bytes 2949124
  30.9 18.1 %collective-permute-start.1 = (bf16[768,640]{1,0:T(8,128)(2,1)}, bf16[768,640]{1,0:T(8,128)(2,1)}, u32[]{:S(2)}, u32[]{:S(2)}) collective-permute-start(bf16[768,640]{1,0:T(8,128)(2,1)} %broadcast_select_fusion), channel_id=1, source_target_pairs={{0,32},{32,64},{64,96},{96,128},{128,160},{160,192},{192,224},{224... | collective-permute-start | bytes 2949128 | tf_op jit(solution)/shard_map/ppermute | solution.py:350
  32.8 16.2 %collective-permute-start.2 = (bf16[768,640]{1,0:T(8,128)(2,1)S(1)}, bf16[768,640]{1,0:T(8,128)(2,1)S(1)}, u32[]{:S(2)}, u32[]{:S(2)}) collective-permute-start(bf16[768,640]{1,0:T(8,128)(2,1)S(1)} %collective-permute-done.near_ref), channel_id=1, source_target_pairs={{0,32},{32,0},{64,96},{96,64},{128,160},{160,128},{192,224},{224,1... | collective-permute-start | bytes 2949128 | tf_op jit(solution)/shard_map/ppermute | solution.py:351
  34.8 14.3 %all-to-all-start.1 = ((f32[16,1,512]{2,1,0:T(1,128)}), f32[16,1,512]{2,1,0:T(1,128)S(1)}, u32[]{:S(2)}, u32[]{:S(2)}) async-start(f32[16,1,512]{2,1,0:T(1,128)} %get-tuple-element.32), calls=%async_computation.1 | async-start | bytes 65536 | tf_op jit(solution)/shard_map/all_to_all | solution.py:352
  49.1 0.6 copy-start.3
  49.1 0.9 copy-start.14
  68.7 20.9 %collective-permute-start.3 = (bf16[768,640]{1,0:T(8,128)(2,1)}, bf16[768,640]{1,0:T(8,128)(2,1)S(1)}, u32[]{:S(2)}, u32[]{:S(2)}) collective-permute-start(bf16[768,640]{1,0:T(8,128)(2,1)} %get-tuple-element.39), channel_id=1, source_target_pairs={{0,32},{32,0},{64,96},{96,64},{128,160},{160,128},{192,224},{224,1... | collective-permute-start | bytes 2949128 | tf_op jit(solution)/shard_map/ppermute | solution.py:359
  70.7 18.9 %collective-permute-start.4 = (bf16[768,640]{1,0:T(8,128)(2,1)}, bf16[768,640]{1,0:T(8,128)(2,1)S(1)}, u32[]{:S(2)}, u32[]{:S(2)}) collective-permute-start(bf16[768,640]{1,0:T(8,128)(2,1)} %get-tuple-element.40), channel_id=1, source_target_pairs={{32,0},{64,32},{96,64},{128,96},{160,128},{192,160},{224,192},{256... | collective-permute-start | bytes 2949128 | tf_op jit(solution)/shard_map/ppermute | solution.py:358
  89.6 6.8 %copy-start.11 = (f32[8,1,768]{2,1,0:T(1,128)S(1)}, f32[8,1,768]{2,1,0:T(1,128)}, u32[]{:S(2)}) copy-start(f32[8,1,768]{2,1,0:T(1,128)} %get-tuple-element.41) | copy-start | bytes 73732
  92.3 33.2 %copy-start.1 = (f32[768,640]{1,0:T(8,128)S(1)}, f32[768,640]{1,0:T(8,128)}, u32[]{:S(2)}) copy-start(f32[768,640]{1,0:T(8,128)} %get-tuple-element.45.k_own.v_own) | copy-start | bytes 5898244
  92.3 33.2 %copy-start.4 = (f32[16,1,512]{2,1,0:T(1,128)S(1)}, f32[16,1,512]{2,1,0:T(1,128)}, u32[]{:S(2)}) copy-start(f32[16,1,512]{2,1,0:T(1,128)} %copy-done.3) | copy-start | bytes 98308
  92.3 33.2 %copy-start.5 = (f32[1,640]{1,0:T(1,128)S(1)}, f32[1,640]{1,0:T(1,128)}, u32[]{:S(2)}) copy-start(f32[1,640]{1,0:T(1,128)} %reshape.17.gain_k_ref.gain_ref) | copy-start | bytes 7684
  92.3 33.2 %copy-start.6 = (s32[3]{0:T(128)S(1)}, s32[3]{0:T(128)}, u32[]{:S(2)}) copy-start(s32[3]{0:T(128)} %pad_add_fusion.tag_ref) | copy-start | bytes 40
  92.3 33.2 %collective-permute-start.5 = (bf16[768,640]{1,0:T(8,128)(2,1)}, bf16[768,640]{1,0:T(8,128)(2,1)}, u32[]{:S(2)}, u32[]{:S(2)}) collective-permute-start(bf16[768,640]{1,0:T(8,128)(2,1)} %add_convert_fusion), channel_id=1, source_target_pairs={{64,0},{96,32},{128,64},{160,96},{192,128},{224,160},{256,192},{28... | collective-permute-start | bytes 2949128 | tf_op jit(solution)/shard_map/ppermute | solution.py:369
  114.5 11.0 %copy-start.2 = (f32[8,1,768]{2,1,0:T(1,128)S(1)}, f32[8,1,768]{2,1,0:T(1,128)}, u32[]{:S(2)}) copy-start(f32[8,1,768]{2,1,0:T(1,128)} %all_to_all.26.inners) | copy-start | bytes 73732
  114.5 14.8 %all-to-all-start.4 = ((f32[4,1,1280]{2,1,0:T(1,128)}), f32[4,1,1280]{2,1,0:T(1,128)S(1)}, u32[]{:S(2)}, u32[]{:S(2)}) async-start(f32[4,1,1280]{2,1,0:T(1,128)} %get-tuple-element.44), calls=%async_computation.4 | async-start | bytes 40960 | tf_op jit(solution)/shard_map/all_to_all | solution.py:372
